TPU v7x, 32 devices: a whole 2x2x4 slice. The times are simulated.
32 devices in a mesh: outer: 8 (over z, x), dp: 2 (over y), mp: 2 (over core).
Axes of the slice: x: 2, y: 2, z: 4, core: 2. Of those that a mesh axis runs over, the one named last changes fastest.
Arguments:
- step_index: int32 [], replicated, may hold values from 0 to 4095
- token_ids: int32 [8, 1024], P('outer', 'dp'), may hold values from 0 to 128255, as said below
- features: bfloat16 [8, 1024, 4096], P('outer', 'dp'), may hold values from -6 to 6
- cotangent: bfloat16 [8, 1024, 2048], P('outer', 'dp', 'mp'), may hold values from -6 to 6
- weight: float32 [8, 4096, 2048], P('outer', 'dp', 'mp'), may hold values from -0.09375 to 0.09375
- momentum: float32 [8, 4096, 2048], P('outer', 'dp', 'mp'), may hold values from -0.3 to 0.3
Outputs:
- input_grad: bfloat16 [8, 1024, 4096], P('outer', 'dp')
- new_weight: float32 [8, 4096, 2048], P('outer', 'dp', 'mp')
- new_momentum: float32 [8, 4096, 2048], P('outer', 'dp', 'mp')
Inputs may be any that keep to these rules, and one draw needn't show every extreme that they name: `token_ids`: the id 128004 marks padding at the end of some blocks of 512 tokens; a quarter of the tokens or so are padding.
All inputs are finite; a program needn't handle non-finite values.
Results may differ from a plain program's by a relative error of at most 0.0049.
Values may be sent and summed in bfloat16 or wider, within the bound.
No kernel may reach another device: no remote copies, remote signals or barrier semaphores. Data moves between devices by JAX's collectives and lax.ppermute only.
A program may use at most 128 MiB of HBM per device.

v0:
```python
import jax
import jax.numpy as jnp
from jax import lax
from jax.sharding import PartitionSpec as P

pad_token = 128004
peak_rate = 0.1
warm_steps = 4096.0
momentum_keep = 0.9


def shortened(x):
    return jax.tree.map(lambda a: a.astype(jnp.bfloat16) if a.dtype == jnp.float32 else a, x)


def from_partner(value, axis, stride):
    mask = 2**stride
    pairs = [(source, source ^ mask) for source in range(lax.axis_size(axis))]
    return lax.ppermute(value, axis, pairs)


def swap_state(values, step_index):
    bit_count = lax.axis_size("outer").bit_length() - 1

    def make_trade(bit_index):

        def trade_with(pair):
            return jax.tree.map(
                lambda part, own: part.astype(own.dtype),
                from_partner(shortened(pair), "outer", bit_index),
                pair,
            )

        return trade_with

    return lax.switch(step_index % bit_count, [make_trade(b) for b in range(bit_count)], values)


def on_device(step_index, token_ids, features, cotangent, weight, momentum):
    activation = features[0]
    tok_rows = activation.shape[0]
    keep_mask = (token_ids[0] != pad_token)[:, None]
    masked = jnp.where(keep_mask, cotangent[0], jnp.zeros_like(cotangent[0]))
    pod_tokens = tok_rows * lax.axis_size("dp")
    master = weight[0]
    velocity_old = momentum[0]
    weight_half = master.astype(jnp.bfloat16)
    rate = peak_rate * (step_index + 1).astype(jnp.float32) / warm_steps
    partial_grad = lax.dot_general(
        masked,
        lax.all_gather(weight_half, "dp", axis=0, tiled=True),
        (((1,), (1,)), ((), ())),
        preferred_element_type=jnp.float32,
    )
    input_grad = lax.psum(partial_grad, "mp").astype(jnp.bfloat16)
    gradient = lax.psum_scatter(
        lax.dot_general(
            activation, masked, (((0,), (0,)), ((), ())), preferred_element_type=jnp.float32
        ),
        "dp",
        scatter_dimension=0,
        tiled=True,
    )
    gradient = gradient / pod_tokens
    velocity = momentum_keep * velocity_old + gradient
    stepped = master - rate * velocity
    peer_stepped, peer_velocity = swap_state((stepped, velocity), step_index)
    new_master = 0.5 * (stepped + peer_stepped)
    new_velocity = 0.5 * (velocity + peer_velocity)
    return (input_grad[None], new_master[None], new_velocity[None])


def solution(mesh):
    placed = (
        P(),
        P("outer", "dp"),
        P("outer", "dp", None),
        P("outer", "dp", "mp"),
        P("outer", "dp", "mp"),
        P("outer", "dp", "mp"),
    )
    return jax.shard_map(
        on_device,
        mesh=mesh,
        in_specs=placed,
        out_specs=(P("outer", "dp", None), P("outer", "dp", "mp"), P("outer", "dp", "mp")),
        check_vma=False,
    )
```

profile of v0, /device:TPU:0, one launch (start us, length us, event | category | flops | bytes accessed | tf_op | source)
XLA Modules:
  0.0 578.3 jit_solution(15245553635375963442)
XLA Ops:
  7.2 0.0 all-gather.2.cloned.1.call-start
  7.2 9.1 %copy.9 = f32[1,2048,1024]{1,2,0:T(8,128)} copy(f32[1,2048,1024]{2,1,0:T(8,128)} %param.13) | data formatting | bytes 16777216 | tf_op args[4]
  16.3 0.0 copy-start
  16.3 0.0 copy-start.1
  16.3 6.1 %bitcast_convert_fusion = bf16[2048,1024]{0,1:T(8,128)(2,1)} fusion(f32[1,2048,1024]{1,2,0:T(8,128)} %copy.9), kind=kLoop, calls=%fused_computation.3 | loop fusion | flops 2097152 | bytes 12582912 | tf_op jit(solution)/shard_map/convert_element_type | solution.py:47
  22.5 0.0 all-gather.2.cloned.1.call-update
  22.5 0.0 reduce-scatter.2.cloned.1.call-start
  22.6 0.0 copy-done
  22.6 0.0 copy-done.1
  22.6 11.3 %convolution_bitcast_fusion = f32[4096,1024]{0,1:T(8,128)} fusion(bf16[1,512,4096]{2,1,0:T(8,128)(2,1)} %param.11, bf16[1,512,1024]{2,1,0:T(8,128)(2,1)S(1)} %copy-done.1, pred[512]{0:T(512)(128)(4,1)S(1)} %compare_reduce_fusion), kind=kOutput, calls=%fused_computation | convolution fusion | flops 4295491584 | bytes 22020608 | tf_op jit(solution)/shard_map/dot_general | solution.py:57
  33.9 0.0 reduce-scatter.2.cloned.1.call-update
  34.6 9.8 %copy.10 = f32[1,2048,1024]{1,2,0:T(8,128)} copy(f32[1,2048,1024]{2,1,0:T(8,128)} %param.14) | data formatting | bytes 16777216 | tf_op args[5]
  44.4 84.9 %all-gather.2.cloned.1.call-done = bf16[4096,1024]{0,1:T(8,128)(2,1)} async-done(((bf16[2048,1024]{0,1:T(8,128)(2,1)}), bf16[4096,1024]{0,1:T(8,128)(2,1)}) %all-gather.2.cloned.1.call-update) | async-done | bytes 8388624 | tf_op jit(solution)/shard_map/all_gather | solution.py:51
  129.4 10.3 %fusion.6 = f32[512,4096]{1,0:T(8,128)} fusion(bf16[4096,1024]{0,1:T(8,128)(2,1)} %all-gather.2.cloned.1.call-done, bf16[1,512,1024]{2,1,0:T(8,128)(2,1)S(1)} %copy-done.1, pred[512]{0:T(512)(128)(4,1)S(1)} %compare_reduce_fusion), kind=kOutput, calls=%fused_computation.14 | convolution fusion | flops 4295491584 | bytes 17826304 | tf_op jit(solution)/shard_map/dot_general | solution.py:49
  139.7 25.5 %all-reduce.1 = bf16[512,4096]{1,0:T(8,128)(2,1)} all-reduce(f32[512,4096]{1,0:T(8,128)} %fusion.6), channel_id=1, replica_groups=mesh['outer'=8,'dp'=2,'mp'=2] {'mp'}, use_global_device_ids=true, to_apply=%region_0.1 | all-reduce | flops 2097152 | bytes 12582912 | tf_op jit(solution)/shard_map/psum | solution.py:55
  165.1 155.7 %reduce-scatter.2.cloned.1.call-done = f32[2048,1024]{0,1:T(8,128)} async-done(((f32[4096,1024]{0,1:T(8,128)}), f32[2048,1024]{0,1:T(8,128)}) %reduce-scatter.2.cloned.1.call-update) | async-done | bytes 8388624 | tf_op jit(solution)/shard_map/reduce_scatter | solution.py:56
  320.8 14.5 %bitcast_subtract_fusion = (f32[2048,1024]{0,1:T(8,128)}, f32[2048,1024]{0,1:T(8,128)}) fusion(f32[1,2048,1024]{1,2,0:T(8,128)} %copy.9, f32[]{:T(128)S(6)} %div.9, f32[2048,1024]{0,1:T(8,128)} %reduce-scatter.2.cloned.1.call-done, f32[1,2048,1024]{1,2,0:T(8,128)} %copy.10), kind=kLoop, calls=%fused_computation.2 | loop fusion | flops 10485760 | bytes 41943044 | tf_op jit(solution)/shard_map/sub | solution.py:66
  335.3 189.9 %conditional.4 = (bf16[2048,1024]{1,0:T(8,128)(2,1)}, bf16[2048,1024]{1,0:T(8,128)(2,1)}) conditional(s32[]{:T(128)} %clamp.3, (f32[2048,1024]{0,1:T(8,128)}, f32[2048,1024]{0,1:T(8,128)}) %bitcast_subtract_fusion, (f32[2048,1024]{0,1:T(8,128)}, f32[2048,1024]{0,1:T(8,128)}) %bitcast_subtract_fusion, (f32[2048,1024]{0,1:T(8,128)}, ...), branch_computations={%region_2.3_spmd, %region_3.4_spmd, %region_4.5_spmd} | conditional | bytes 58720352
  335.3 7.4 %copy.11 = bf16[2048,1024]{1,0:T(8,128)(2,1)} copy(f32[2048,1024]{0,1:T(8,128)} %get-tuple-element.41) | data formatting | bytes 12582912 | tf_op jit(solution)/shard_map
  342.7 1.5 collective-permute-start
  344.2 7.3 %copy.12 = bf16[2048,1024]{1,0:T(8,128)(2,1)} copy(f32[2048,1024]{0,1:T(8,128)} %get-tuple-element.42) | data formatting | bytes 12582912 | tf_op jit(solution)/shard_map
  351.5 0.6 collective-permute-start.1
  352.0 84.4 %collective-permute-done = bf16[2048,1024]{1,0:T(8,128)(2,1)} collective-permute-done((bf16[2048,1024]{1,0:T(8,128)(2,1)}, bf16[2048,1024]{1,0:T(8,128)(2,1)}, u32[]{:S(2)}, u32[]{:S(2)}) %collective-permute-start) | collective-permute-done | bytes 4194336 | tf_op jit(solution)/shard_map/cond/branch_0_fun/ppermute | solution.py:19
  436.5 88.7 %collective-permute-done.1 = bf16[2048,1024]{1,0:T(8,128)(2,1)} collective-permute-done((bf16[2048,1024]{1,0:T(8,128)(2,1)}, bf16[2048,1024]{1,0:T(8,128)(2,1)}, u32[]{:S(2)}, u32[]{:S(2)}) %collective-permute-start.1) | collective-permute-done | bytes 4194336 | tf_op jit(solution)/shard_map/cond/branch_0_fun/ppermute | solution.py:19
  525.2 6.5 %copy.18 = bf16[2048,1024]{0,1:T(8,128)(2,1)} copy(bf16[2048,1024]{1,0:T(8,128)(2,1)} %get-tuple-element.40) | data formatting | bytes 8388608
  531.7 6.5 %copy.17 = bf16[2048,1024]{0,1:T(8,128)(2,1)} copy(bf16[2048,1024]{1,0:T(8,128)(2,1)} %get-tuple-element.39) | data formatting | bytes 8388608
  538.1 14.8 %fusion.1 = (f32[1,2048,1024]{1,2,0:T(8,128)}, f32[1,2048,1024]{1,2,0:T(8,128)}) fusion(f32[2048,1024]{0,1:T(8,128)} %get-tuple-element.51, bf16[2048,1024]{0,1:T(8,128)(2,1)} %copy.18, f32[2048,1024]{0,1:T(8,128)} %get-tuple-element.50, bf16[2048,1024]{0,1:T(8,128)(2,1)} %copy.17), kind=kLoop, calls=%fused_computation.6 | loop fusion | flops 12582912 | bytes 41943040 | tf_op jit(solution)/shard_map/broadcast_in_dim | solution.py:70
  553.0 9.2 %copy.19 = f32[1,2048,1024]{2,1,0:T(8,128)} copy(f32[1,2048,1024]{1,2,0:T(8,128)} %get-tuple-element.53) | data formatting | bytes 16777216
  562.2 9.2 %copy.20 = f32[1,2048,1024]{2,1,0:T(8,128)} copy(f32[1,2048,1024]{1,2,0:T(8,128)} %get-tuple-element.52) | data formatting | bytes 16777216
  (1 shorter events, 0.0 us)
Async XLA Ops:
  7.2 122.2 %all-gather.2.cloned.1.call-start = ((), (), s32[]{:S(2)}) async-start(), calls=%async_computation.1 | async-start | bytes 12582912 | tf_op jit(solution)/shard_map/all_gather | solution.py:51
  16.3 6.2 %copy-start = (s32[1,512]{1,0:T(1,128)S(1)}, s32[1,512]{1,0:T(1,128)}, u32[]{:S(2)}) copy-start(s32[1,512]{1,0:T(1,128)} %param.10) | copy-start | bytes 6148
  16.3 6.2 %copy-start.1 = (bf16[1,512,1024]{2,1,0:T(8,128)(2,1)S(1)}, bf16[1,512,1024]{2,1,0:T(8,128)(2,1)}, u32[]{:S(2)}) copy-start(bf16[1,512,1024]{2,1,0:T(8,128)(2,1)} %param.12) | copy-start | bytes 3145732
  22.5 298.3 %reduce-scatter.2.cloned.1.call-start = ((), (), s32[]{:S(2)}) async-start(), calls=%async_computation.2 | async-start | bytes 25165824 | tf_op jit(solution)/shard_map/reduce_scatter | solution.py:56
  342.7 93.8 %collective-permute-start = (bf16[2048,1024]{1,0:T(8,128)(2,1)}, bf16[2048,1024]{1,0:T(8,128)(2,1)}, u32[]{:S(2)}, u32[]{:S(2)}) collective-permute-start(bf16[2048,1024]{1,0:T(8,128)(2,1)} %copy.11), channel_id=1, source_target_pairs={{0,4},{4,0},{8,12},{12,8},{16,20},{20,16},{24,28},{28,24},{1,5},{5... | collective-permute-start | bytes 12582920 | tf_op jit(solution)/shard_map/cond/branch_0_fun/ppermute | solution.py:19
  351.5 173.7 %collective-permute-start.1 = (bf16[2048,1024]{1,0:T(8,128)(2,1)}, bf16[2048,1024]{1,0:T(8,128)(2,1)}, u32[]{:S(2)}, u32[]{:S(2)}) collective-permute-start(bf16[2048,1024]{1,0:T(8,128)(2,1)} %copy.12), channel_id=1, source_target_pairs={{0,4},{4,0},{8,12},{12,8},{16,20},{20,16},{24,28},{28,24},{1,5},{5... | collective-permute-start | bytes 12582920 | tf_op jit(solution)/shard_map/cond/branch_0_fun/ppermute | solution.py:19
Sparse Core Ops, SparseCore 0:
  22.6 106.6 all-gather.1
  131.7 189.1 reduce-scatter.1
where the time goes:
time: 579 us; the launch traced here: 578 us
  waiting for transfers between devices  414 us (72%)
  local copies, waits for them, and re-layouts  65.1 us (11%)
  other arithmetic  35.5 us (6%)
  blocking collectives  25.5 us (4%)
  matrix products  21.6 us (4%)
  between operations  14.7 us (3%)
    ppermute x2, waiting for transfers between devices, from_partner(): return lax.ppermute(value, axis, pairs)  173 us
    reduce_scatter x1, waiting for transfers between devices, on_device(): lax.psum_scatter(lax.dot_general(activation, masked, (((0,), (0,)), ((),...  156 us
    all_gather x1, waiting for transfers between devices, on_device(): lax.all_gather(weight_half, 'dp', axis=0, tiled=True)  84.9 us
    unnamed x10, local copies, waits for them, and re-layouts  50.4 us
    psum x1, blocking collectives, on_device(): input_grad = lax.psum(partial_grad, 'mp').astype(jnp.bfloat16)  25.5 us
    broadcast_in_dim x1, other arithmetic, on_device(): return (input_grad[None], new_master[None], new_velocity[None])  14.8 us
    another operation x2, local copies, waits for them, and re-layouts  14.7 us
    sub x1, other arithmetic, on_device(): stepped = master - rate * velocity  14.5 us
  transfers between devices with their start and end apart: 4, of which 4 were waited for; matrix products, arithmetic and copies ran while one was open for 7% of the time, Pallas kernels for 0%

commit v1 on v0

v1 whole, which is shorter than its diff:
```python
import functools

import jax
import jax.numpy as jnp
from jax import lax
from jax.experimental import pallas as pl
from jax.experimental.pallas import tpu as pltpu
from jax.sharding import PartitionSpec as P

pad_token = 128004
peak_rate = 0.1
warm_steps = 4096.0
momentum_keep = 0.9

velocity_parts = (10, 4, 1, 1)

any_spec = pl.BlockSpec(memory_space=pl.ANY)


def shifted(value, axis, by):
    n = lax.axis_size(axis)
    return lax.ppermute(value, axis, [(s, (s + by) % n) for s in range(n)])


def from_partner(value, bit):
    n = lax.axis_size("outer")
    return lax.ppermute(value, "outer", [(s, s ^ (1 << bit)) for s in range(n)])


def starts_of(parts, rows):
    out, at, upto = [], 0, 0
    for part in parts:
        upto += part
        end = -(-rows * upto // (16 * 128)) * 128
        if end > at:
            out.append((at, end - at))
        at = end
    return out


def fitting(largest, *sizes):
    block = largest
    while any(size % block for size in sizes):
        block //= 2
    return block


class Chain:
    def __init__(self):
        self.token = None

    def call(self, kernel, name, grid, places, ins, outs, aliases=()):
        ins = list(ins)
        n_out = len(outs)
        if self.token is not None:
            ins.append((self.token, any_spec))
        n_in = len(ins)

        def body(place_ref, *refs):
            kernel(place_ref, refs[:n_in], refs[n_in : n_in + n_out])

        got = pl.pallas_call(
            body,
            grid_spec=pltpu.PrefetchScalarGridSpec(
                num_scalar_prefetch=1,
                grid=grid,
                in_specs=[spec for _, spec in ins],
                out_specs=[spec for _, _, spec in outs] + [any_spec],
            ),
            out_shape=[jax.ShapeDtypeStruct(shape, kind) for shape, kind, _ in outs]
            + [jax.ShapeDtypeStruct((8, 128), jnp.float32)],
            input_output_aliases={i + 1: o for i, o in aliases},
            compiler_params=pltpu.CompilerParams(vmem_limit_bytes=63 * 1024 * 1024),
            cost_estimate=pl.CostEstimate(flops=0, bytes_accessed=0, transcendentals=0),
            name=name,
        )(places, *[array for array, _ in ins])
        self.token = got[-1]
        return got[:-1]


def cast_kernel(places, ins, outs):
    outs[0][...] = ins[0][...].astype(outs[0].dtype)


def cast_rows(chain, places, weight):
    rows, cols = weight.shape
    block = fitting(256, rows)
    spec = pl.BlockSpec((block, cols), lambda r, at: (r, 0))
    return chain.call(
        cast_kernel,
        "cast_rows",
        (rows // block,),
        places,
        [(weight, spec)],
        [((rows, cols), jnp.bfloat16, spec)],
    )[0]


def mask_kernel(places, ins, outs):
    ids, cot = ins[0], ins[1]
    rows, cols = cot.shape
    turned = jnp.broadcast_to(ids[...], (128, rows)).T
    keep = turned != pad_token
    for at in range(0, cols, 128):
        value = cot[:, at : at + 128]
        outs[0][:, at : at + 128] = jnp.where(keep, value, jnp.zeros_like(value))


def mask_rows(chain, places, ids, cot):
    rows, cols = cot.shape
    block = fitting(256, rows)
    return chain.call(
        mask_kernel,
        "mask_rows",
        (rows // block,),
        places,
        [
            (ids, pl.BlockSpec((1, block), lambda r, at: (0, r))),
            (cot, pl.BlockSpec((block, cols), lambda r, at: (r, 0))),
        ],
        [((rows, cols), cot.dtype, pl.BlockSpec((block, cols), lambda r, at: (r, 0)))],
    )[0]


def take_columns(chain, places, features, by, n, half):
    toks = features.shape[0]
    block = fitting(256, toks)
    return chain.call(
        cast_kernel,
        "take_columns",
        (toks // block,),
        places,
        [
            (
                features,
                pl.BlockSpec((block, half), lambda r, at: (r, 2 * lax.rem(at[0] + by, n) + at[1])),
            )
        ],
        [((toks, half), features.dtype, pl.BlockSpec((block, half), lambda r, at: (r, 0)))],
    )[0]


def take_rows(chain, places, short):
    half, cols = short.shape[0] // 2, short.shape[1]
    block = fitting(512, half)
    steps = half // block
    return chain.call(
        cast_kernel,
        "take_rows",
        (steps,),
        places,
        [(short, pl.BlockSpec((block, cols), lambda r, at: ((1 - at[1]) * steps + r, 0)))],
        [((half, cols), short.dtype, pl.BlockSpec((block, cols), lambda r, at: (r, 0)))],
    )[0]


def velocity_kernel(n, scale, places, ins, outs):
    total = None
    for x_ref, m_ref in zip(ins[:n], ins[n : 2 * n]):
        term = lax.dot_general(
            x_ref[...], m_ref[...], (((0,), (0,)), ((), ())), preferred_element_type=jnp.float32
        )
        total = term if total is None else total + term
    v = momentum_keep * ins[2 * n][...] + total * scale
    outs[0][...] = v
    outs[1][...] = v.astype(jnp.bfloat16)


def velocity_rows(chain, places, activation, others, masks, momentum, first, size):
    rows, cols = momentum.shape
    toks = activation.shape[0]
    n = len(masks)
    block = fitting(256, first, size)
    per_dev, skip = rows // block, first // block
    row_spec = pl.BlockSpec((block, cols), lambda r, at: (r, 0))
    return chain.call(
        functools.partial(velocity_kernel, n, 1.0 / (toks * n)),
        "velocity_rows",
        (size // block,),
        places,
        [(activation, pl.BlockSpec((toks, block), lambda r, at: (0, at[0] * per_dev + skip + r)))]
        + [(x, pl.BlockSpec((toks, block), lambda r, at: (0, skip + r))) for x in others]
        + [(m, pl.BlockSpec((toks, cols), lambda r, at: (0, 0))) for m in masks]
        + [(momentum, pl.BlockSpec((block, cols), lambda r, at: (skip + r, 0)))],
        [((size, cols), jnp.float32, row_spec), ((size, cols), jnp.bfloat16, row_spec)],
    )


def input_kernel(places, ins, outs):
    own, other = (
        lax.dot_general(
            ins[at][...], ins[at + 1][...], (((1,), (1,)), ((), ())), preferred_element_type=jnp.float32
        )
        for at in (0, 2)
    )
    outs[0][...] = (own + other).astype(outs[0].dtype)


def input_columns(chain, places, mask, short, mask_other, short_other):
    half, cols = short_other.shape
    toks = mask.shape[0]
    block = fitting(256, half)
    steps = half // block
    mask_spec = pl.BlockSpec((toks, cols), lambda r, at: (0, 0))
    return chain.call(
        input_kernel,
        "input_columns",
        (steps,),
        places,
        [
            (mask, mask_spec),
            (short, pl.BlockSpec((block, cols), lambda r, at: (at[1] * steps + r, 0))),
            (mask_other, mask_spec),
            (short_other, pl.BlockSpec((block, cols), lambda r, at: (r, 0))),
        ],
        [((toks, half), jnp.bfloat16, pl.BlockSpec((toks, block), lambda r, at: (0, r)))],
    )[0]


def join_kernel(n, places, ins, outs):
    column = pl.program_id(0)
    by = lax.rem(column // 2 - places[0] + n, n)
    piece = 2 * by + jnp.where(lax.rem(column, 2) == places[1], 0, 1)
    for at in range(2 * n):

        @pl.when(piece == at)
        def _():
            outs[0][...] = ins[at][...]


def join_columns(chain, places, pieces):
    toks, width = pieces[0].shape
    return chain.call(
        functools.partial(join_kernel, len(pieces) // 2),
        "join_columns",
        (len(pieces),),
        places,
        [(piece, pl.BlockSpec((toks, width), lambda c, at: (0, 0))) for piece in pieces],
        [
            (
                (toks, width * len(pieces)),
                pieces[0].dtype,
                pl.BlockSpec((toks, width), lambda c, at: (0, c)),
            )
        ],
    )[0]


def half_kernel(places, ins, outs):
    outs[0][...] = 0.5 * (ins[0][...] + ins[1][...].astype(jnp.float32))


def half_rows(chain, places, weight, peer):
    rows, cols = weight.shape
    block = fitting(256, rows)
    spec = pl.BlockSpec((block, cols), lambda r, at: (r, 0))
    return chain.call(
        half_kernel,
        "half_rows",
        (rows // block,),
        places,
        [(weight, spec), (peer, spec)],
        [((rows, cols), jnp.float32, spec)],
    )[0]


def final_kernel(places, ins, outs):
    mean = 0.5 * (ins[0][...] + ins[1][...].astype(jnp.float32))
    outs[1][...] = mean
    outs[0][...] = ins[2][...] - ins[3][0] * mean


def final_rows(chain, places, rate, v, peer, half, into, first):
    rows, cols = half.shape
    size = v.shape[0]
    block = fitting(256, first, size)
    skip = first // block
    part_spec = pl.BlockSpec((block, cols), lambda r, at: (r, 0))
    whole_spec = pl.BlockSpec((block, cols), lambda r, at: (skip + r, 0))
    ins = [
        (v, part_spec),
        (peer, part_spec),
        (half, whole_spec),
        (rate, pl.BlockSpec(memory_space=pltpu.SMEM)),
    ]
    aliases = [(2, 0)]
    if into is not None:
        aliases.append((len(ins), 1))
        ins.append((into, any_spec))
    return chain.call(
        final_kernel,
        "final_rows",
        (size // block,),
        places,
        ins,
        [((rows, cols), jnp.float32, whole_spec)] * 2,
        aliases,
    )


def step_with(bit, places, rate, ids, activation, cotangent, weight, momentum):
    rows = weight.shape[0]
    n_dp = lax.axis_size("dp")
    mp = places[1]
    half = rows // 2
    chain = Chain()

    short = cast_rows(chain, places, weight)
    weight_peer = from_partner(short, bit)

    masked = mask_rows(chain, places, ids, cotangent)
    masks = [masked] + [shifted(masked, "dp", k) for k in range(1, n_dp)]

    others = []
    for k in range(1, n_dp):
        mine = shifted(take_columns(chain, places, activation, k, n_dp, half), "dp", k)
        other = shifted(mine, "mp", 1)
        others.append(
            jnp.where(mp == 0, jnp.concatenate([mine, other], 1), jnp.concatenate([other, mine], 1))
        )

    short_other = shifted(take_rows(chain, places, short), "mp", 1)

    velocities = []
    for first, size in starts_of(velocity_parts, rows):
        v, v_short = velocity_rows(chain, places, activation, others, masks, momentum, first, size)
        velocities.append((first, v, from_partner(v_short, bit)))

    new_weight = half_rows(chain, places, weight, weight_peer)

    done = {}
    for k in reversed(range(n_dp)):
        done[k] = input_columns(
            chain, places, masks[k], short, shifted(masks[k], "mp", 1), short_other
        )
        if k:
            done[k] = shifted(done[k], "dp", n_dp - k)

    pieces = []
    for k in range(n_dp):
        pieces += [done[k], shifted(done[k], "mp", 1)]
    input_grad = join_columns(chain, places, pieces)

    new_momentum = None
    for first, v, peer in velocities:
        new_weight, new_momentum = final_rows(
            chain, places, rate, v, peer, new_weight, new_momentum, first
        )
    return input_grad, new_weight, new_momentum


def on_device(step_index, token_ids, features, cotangent, weight, momentum):
    bit_count = lax.axis_size("outer").bit_length() - 1
    places = jnp.stack([lax.axis_index("dp"), lax.axis_index("mp")]).astype(jnp.int32)
    rate = (peak_rate * (step_index + 1).astype(jnp.float32) / warm_steps)[None]
    outs = lax.switch(
        step_index % bit_count,
        [functools.partial(step_with, bit) for bit in range(bit_count)],
        places,
        rate,
        token_ids,
        features[0],
        cotangent[0],
        weight[0],
        momentum[0],
    )
    return tuple(out[None] for out in outs)


def solution(mesh):
    placed = (
        P(),
        P("outer", "dp"),
        P("outer", "dp", None),
        P("outer", "dp", "mp"),
        P("outer", "dp", "mp"),
        P("outer", "dp", "mp"),
    )
    return jax.shard_map(
        on_device,
        mesh=mesh,
        in_specs=placed,
        out_specs=(P("outer", "dp", None), P("outer", "dp", "mp"), P("outer", "dp", "mp")),
        check_vma=False,
    )
```

time: 579 us -> 198 us (0.34)
  waiting for transfers between devices: 414 us -> 88.5 us
  Pallas kernels: 0 us -> 90.8 us
  local copies, waits for them, and re-layouts: 65.1 us -> 1.39 us
  other arithmetic: 35.5 us -> 3.75 us
  blocking collectives: 25.5 us -> 0 us
  matrix products: 21.6 us -> 0 us
  between operations: 14.7 us -> 1.48 us
  starting transfers between devices: 2.11 us -> 11.1 us
    reduce_scatter x1 -> x0, waiting for transfers between devices: 156 us -> none  [on_device(): lax.psum_scatter(lax.dot_general(activation, masked, (((0,), (0,)), ((),...]
    pallas_call x0 -> x16, Pallas kernels: none -> 90.8 us  [call(): pl.pallas_call(body, grid_spec=pltpu.PrefetchScalarGridSpec(num_scalar_pr...]
    all_gather x1 -> x0, waiting for transfers between devices: 84.9 us -> none  [on_device(): lax.all_gather(weight_half, 'dp', axis=0, tiled=True)]
    ppermute x2 -> x14, waiting for transfers between devices: 173 us -> 88.5 us  [the longest x9 57.2 us: shifted(): return lax.ppermute(value, axis, [(s, (s + by) % n) for s in range(n)])]
    unnamed x10 -> x0, local copies, waits for them, and re-layouts: 50.4 us -> none
    psum x1 -> x0, blocking collectives: 25.5 us -> none  [on_device(): input_grad = lax.psum(partial_grad, 'mp').astype(jnp.bfloat16)]
    dot_general x2 -> x0, matrix products: 21.6 us -> none  [the longest x1 11.3 us: on_device(): lax.dot_general(activation, masked, (((0,), (0,)), ((), ())), preferred_e...]
    broadcast_in_dim x1 -> x0, other arithmetic: 14.8 us -> none  [on_device(): return (input_grad[None], new_master[None], new_velocity[None])]
  transfers between devices with their start and end apart: 4 -> 14, of which waited for: 4 -> 8; matrix products, arithmetic and copies ran while one was open for 7% -> 2% of each run, Pallas kernels for 0% -> 40%
where the time goes in v1:
time: 198 us
  Pallas kernels  90.8 us (46%)
  waiting for transfers between devices  88.5 us (45%)
  starting transfers between devices  11.1 us (6%)
  other arithmetic  3.75 us (2%)
    pallas_call x16, Pallas kernels, call(): pl.pallas_call(body, grid_spec=pltpu.PrefetchScalarGridSpec(num_scalar_pr...  90.8 us
    ppermute x9, waiting for transfers between devices, shifted(): return lax.ppermute(value, axis, [(s, (s + by) % n) for s in range(n)])  57.2 us
    ppermute x5, waiting for transfers between devices, from_partner(): return lax.ppermute(value, 'outer', [(s, s ^ 1 << bit) for s in range(n)])  31.3 us
    ppermute x5, starting transfers between devices, from_partner(): return lax.ppermute(value, 'outer', [(s, s ^ 1 << bit) for s in range(n)])  6.76 us
    ppermute x9, starting transfers between devices, shifted(): return lax.ppermute(value, axis, [(s, (s + by) % n) for s in range(n)])  4.33 us
  transfers between devices with their start and end apart: 14, of which 8 were waited for; matrix products, arithmetic and copies ran while one was open for 2% of the time, Pallas kernels for 40%

profile of v1, /device:TPU:0, one launch (start us, length us, event | category | flops | bytes accessed | tf_op | source)
XLA Modules:
  0.0 197.7 jit_solution(12515558751952461134)
XLA Ops:
  1.4 196.1 %conditional.1 = (bf16[512,4096]{1,0:T(8,128)(2,1)}, f32[2048,1024]{1,0:T(8,128)}, f32[2048,1024]{1,0:T(8,128)}) conditional(s32[]{:T(128)} %clamp.3, (s32[2]{0:T(128)S(1)}, f32[2048,1024]{1,0:T(8,128)}, s32[1,512]{1,0:T(1,128)}, bf16[512,1024]{1,0:T(8,128)(2,1)}, bf16[512,4096]{1,0:T(8,128)(2,1)}, /*index=5*/s32[]{:T(128)}, ...), branch_computations={%region_0.1_spmd, %region_1.2_spmd, %region_2.3_spmd} | conditional | flops 9437185 | bytes 82846400 | solution.py:356
  1.6 8.2 %cast_rows.4 = (bf16[2048,1024]{1,0:T(8,128)(2,1)}, f32[8,128]{1,0:T(8,128)}) custom-call(s32[2]{0:T(128)S(1)} %get-tuple-element.95.place_ref, f32[2048,1024]{1,0:T(8,128)} %get-tuple-element.98.refs_0_), custom_call_target="tpu_custom_call" | custom-call | tf_op jit(solution)/shard_map/cond/branch_1_fun/cast_rows/pallas_call | solution.py:62
  9.8 3.0 %collective-permute-start.18 = (bf16[2048,1024]{1,0:T(8,128)(2,1)}, bf16[2048,1024]{1,0:T(8,128)(2,1)}, u32[]{:S(2)}, u32[]{:S(2)}) collective-permute-start(bf16[2048,1024]{1,0:T(8,128)(2,1)} %get-tuple-element.101.refs_0_.refs_1_), channel_id=1, source_target_pairs={{0,8},{4,12},{8,0},{12,4},{16,24},{20,28},{24,16},{28,20},{1,9},{5... | collective-permute-start | bytes 12582920 | tf_op jit(solution)/shard_map/cond/branch_1_fun/ppermute | solution.py:27
  12.9 2.8 %mask_rows.4 = (bf16[512,1024]{1,0:T(8,128)(2,1)}, f32[8,128]{1,0:T(8,128)}) custom-call(s32[2]{0:T(128)S(1)} %get-tuple-element.95.place_ref, s32[1,512]{1,0:T(1,128)S(1)} %copy-done.7, bf16[512,1024]{1,0:T(8,128)(2,1)} %get-tuple-element.97.refs_1_, f32[8,128]{1,0:T(8,128)} %get-tuple-element.99.refs_2_), custom_call_target="tpu_custom_call" | custom-call | tf_op jit(solution)/shard_map/cond/branch_1_fun/mask_rows/pallas_call | solution.py:62
  15.6 2.6 %take_columns.4 = (bf16[512,1024]{1,0:T(8,128)(2,1)}, f32[8,128]{1,0:T(8,128)}) custom-call(s32[2]{0:T(128)S(1)} %get-tuple-element.95.place_ref, bf16[512,4096]{1,0:T(8,128)(2,1)} %get-tuple-element.102.refs_0_, f32[8,128]{1,0:T(8,128)} %get-tuple-element.103.refs_1_), custom_call_target="tpu_custom_call" | custom-call | tf_op jit(solution)/shard_map/cond/branch_1_fun/take_columns/pallas_call | solution.py:62
  18.2 1.5 collective-permute-start.19
  20.3 3.2 %take_rows.4 = (bf16[1024,1024]{1,0:T(8,128)(2,1)}, f32[8,128]{1,0:T(8,128)}) custom-call(s32[2]{0:T(128)S(1)} %get-tuple-element.95.place_ref, bf16[2048,1024]{1,0:T(8,128)(2,1)} %get-tuple-element.101.refs_0_.refs_1_, f32[8,128]{1,0:T(8,128)} %get-tuple-element.104.refs_1_), custom_call_target="tpu_custom_call" | custom-call | tf_op jit(solution)/shard_map/cond/branch_1_fun/take_rows/pallas_call | solution.py:62
  23.4 21.2 %collective-permute-done.19 = bf16[512,1024]{1,0:T(8,128)(2,1)} collective-permute-done((bf16[512,1024]{1,0:T(8,128)(2,1)}, bf16[512,1024]{1,0:T(8,128)(2,1)}, u32[]{:S(2)}, u32[]{:S(2)}) %collective-permute-start.19) | collective-permute-done | bytes 1048608 | tf_op jit(solution)/shard_map/cond/branch_1_fun/ppermute | solution.py:22
  44.6 21.0 %collective-permute-done.16.refs_3_.refs_0_ = bf16[512,1024]{1,0:T(8,128)(2,1)} collective-permute-done((bf16[512,1024]{1,0:T(8,128)(2,1)}, bf16[512,1024]{1,0:T(8,128)(2,1)}, u32[]{:S(2)}, u32[]{:S(2)}) %collective-permute-start.16) | collective-permute-done | bytes 1048608 | tf_op jit(solution)/shard_map/cond/branch_1_fun/ppermute | solution.py:22
  65.6 3.7 %maximum_select_fusion.1.refs_1_ = bf16[512,2048]{1,0:T(8,128)(2,1)} fusion(bf16[512,1024]{1,0:T(8,128)(2,1)S(1)} %collective-permute-done.20, bf16[512,1024]{1,0:T(8,128)(2,1)} %collective-permute-done.19, pred[]{:T(512)S(6)} %eq.9), kind=kLoop, calls=%fused_computation.1 | loop fusion | flops 9437184 | bytes 4194305 | tf_op jit(solution)/shard_map/cond/branch_1_fun/jit(_where)/select_n | solution.py:319
  69.3 11.1 %velocity_rows.16 = (f32[1280,1024]{1,0:T(8,128)}, bf16[1280,1024]{1,0:T(8,128)(2,1)}, f32[8,128]{1,0:T(8,128)}) custom-call(s32[2]{0:T(128)S(1)} %get-tuple-element.95.place_ref, bf16[512,4096]{1,0:T(8,128)(2,1)} %get-tuple-element.102.refs_0_, bf16[512,2048]{1,0:T(8,128)(2,1)} %maximum_select_fusion.1.refs_1_, ...), custom_call_target="tpu_custom_call" | custom-call | tf_op jit(solution)/shard_map/cond/branch_1_fun/velocity_rows/pallas_call | solution.py:62
  81.0 5.3 %velocity_rows.17 = (f32[512,1024]{1,0:T(8,128)}, bf16[512,1024]{1,0:T(8,128)(2,1)}, f32[8,128]{1,0:T(8,128)}) custom-call(s32[2]{0:T(128)S(1)} %get-tuple-element.95.place_ref, bf16[512,4096]{1,0:T(8,128)(2,1)} %get-tuple-element.102.refs_0_, bf16[512,2048]{1,0:T(8,128)(2,1)} %maximum_select_fusion.1.refs_1_, ...), custom_call_target="tpu_custom_call" | custom-call | tf_op jit(solution)/shard_map/cond/branch_1_fun/velocity_rows/pallas_call | solution.py:62
  86.3 3.8 %velocity_rows.18 = (f32[128,1024]{1,0:T(8,128)}, bf16[128,1024]{1,0:T(8,128)(2,1)}, f32[8,128]{1,0:T(8,128)}) custom-call(s32[2]{0:T(128)S(1)} %get-tuple-element.95.place_ref, bf16[512,4096]{1,0:T(8,128)(2,1)} %get-tuple-element.102.refs_0_, bf16[512,2048]{1,0:T(8,128)(2,1)} %maximum_select_fusion.1.refs_1_, ...), custom_call_target="tpu_custom_call" | custom-call | tf_op jit(solution)/shard_map/cond/branch_1_fun/velocity_rows/pallas_call | solution.py:62
  90.1 3.7 %velocity_rows.19 = (f32[128,1024]{1,0:T(8,128)}, bf16[128,1024]{1,0:T(8,128)(2,1)}, f32[8,128]{1,0:T(8,128)}) custom-call(s32[2]{0:T(128)S(1)} %get-tuple-element.95.place_ref, bf16[512,4096]{1,0:T(8,128)(2,1)} %get-tuple-element.102.refs_0_, bf16[512,2048]{1,0:T(8,128)(2,1)} %maximum_select_fusion.1.refs_1_, ...), custom_call_target="tpu_custom_call" | custom-call | tf_op jit(solution)/shard_map/cond/branch_1_fun/velocity_rows/pallas_call | solution.py:62
  93.8 10.7 %collective-permute-done.18.refs_1_ = bf16[2048,1024]{1,0:T(8,128)(2,1)} collective-permute-done((bf16[2048,1024]{1,0:T(8,128)(2,1)}, bf16[2048,1024]{1,0:T(8,128)(2,1)}, u32[]{:S(2)}, u32[]{:S(2)}) %collective-permute-start.18) | collective-permute-done | bytes 4194336 | tf_op jit(solution)/shard_map/cond/branch_1_fun/ppermute | solution.py:27
  104.6 10.3 %half_rows.4 = (f32[2048,1024]{1,0:T(8,128)}, f32[8,128]{1,0:T(8,128)}) custom-call(s32[2]{0:T(128)S(1)} %get-tuple-element.95.place_ref, f32[2048,1024]{1,0:T(8,128)} %get-tuple-element.98.refs_0_, bf16[2048,1024]{1,0:T(8,128)(2,1)} %collective-permute-done.18.refs_1_, f32[8,128]{1,0:T(8,128)} %get-tuple-element.113.refs_2_), custom_call_target="tpu_custom_call" | custom-call | tf_op jit(solution)/shard_map/cond/branch_1_fun/half_rows/pallas_call | solution.py:62
  114.9 6.8 %input_columns.8 = (bf16[512,1024]{1,0:T(8,128)(2,1)}, f32[8,128]{1,0:T(8,128)}) custom-call(s32[2]{0:T(128)S(1)} %get-tuple-element.95.place_ref, bf16[512,1024]{1,0:T(8,128)(2,1)} %collective-permute-done.16.refs_3_.refs_0_, bf16[2048,1024]{1,0:T(8,128)(2,1)} %get-tuple-element.101.refs_0_.refs_1_, bf16[512,1024]{1,0:T(8,128)(2,1)} %collective-permute-done.17.refs_2_, ...), custom_call_target="tpu_custom_call" | custom-call | tf_op jit(solution)/shard_map/cond/branch_1_fun/input_columns/pallas_call | solution.py:62
  121.7 2.0 %collective-permute-start.22 = (bf16[512,1024]{1,0:T(8,128)(2,1)}, bf16[512,1024]{1,0:T(8,128)(2,1)}, u32[]{:S(2)}, u32[]{:S(2)}) collective-permute-start(bf16[512,1024]{1,0:T(8,128)(2,1)} %get-tuple-element.117), channel_id=1, source_target_pairs={{0,2},{2,0},{1,3},{3,1},{4,6},{6,4},{5,7},{7,5},{8,10},{10,8},{9,1... | collective-permute-start | bytes 3145736 | tf_op jit(solution)/shard_map/cond/branch_1_fun/ppermute | solution.py:22
  123.7 6.8 %input_columns.9 = (bf16[512,1024]{1,0:T(8,128)(2,1)}, f32[8,128]{1,0:T(8,128)}) custom-call(s32[2]{0:T(128)S(1)} %get-tuple-element.95.place_ref, bf16[512,1024]{1,0:T(8,128)(2,1)} %get-tuple-element.100.refs_2_.refs_0_, bf16[2048,1024]{1,0:T(8,128)(2,1)} %get-tuple-element.101.refs_0_.refs_1_, bf16[512,1024]{1,0:T(8,128)(2,1)} %collective-permute-done.14.refs_2_, ...), custom_call_target="tpu_custom_call" | custom-call | tf_op jit(solution)/shard_map/cond/branch_1_fun/input_columns/pallas_call | solution.py:62
  130.6 15.0 %collective-permute-done.22.refs_2_ = bf16[512,1024]{1,0:T(8,128)(2,1)} collective-permute-done((bf16[512,1024]{1,0:T(8,128)(2,1)}, bf16[512,1024]{1,0:T(8,128)(2,1)}, u32[]{:S(2)}, u32[]{:S(2)}) %collective-permute-start.22) | collective-permute-done | bytes 1048608 | tf_op jit(solution)/shard_map/cond/branch_1_fun/ppermute | solution.py:22
  145.6 1.4 collective-permute-start.26
  147.6 1.4 collective-permute-start.24
  149.0 5.2 %join_columns.4 = (bf16[512,4096]{1,0:T(8,128)(2,1)}, f32[8,128]{1,0:T(8,128)}) custom-call(s32[2]{0:T(128)S(1)} %get-tuple-element.95.place_ref, bf16[512,1024]{1,0:T(8,128)(2,1)} %get-tuple-element.116.refs_0_, bf16[512,1024]{1,0:T(8,128)(2,1)} %collective-permute-done.21.refs_1_, bf16[512,1024]{1,0:T(8,128)(2,1)} %collective-permute-done.22.refs_2_, ...), custom_call_target="tpu_custom_call" | custom-call | tf_op jit(solution)/shard_map/cond/branch_1_fun/join_columns/pallas_call | solution.py:62
  154.2 6.5 %collective-permute-done.27.refs_1_ = bf16[1280,1024]{1,0:T(8,128)(2,1)} collective-permute-done((bf16[1280,1024]{1,0:T(8,128)(2,1)}, bf16[1280,1024]{1,0:T(8,128)(2,1)}, u32[]{:S(2)}, u32[]{:S(2)}) %collective-permute-start.27) | collective-permute-done | bytes 2621472 | tf_op jit(solution)/shard_map/cond/branch_1_fun/ppermute | solution.py:27
  160.7 10.7 %final_rows.16 = (f32[2048,1024]{1,0:T(8,128)}, f32[2048,1024]{1,0:T(8,128)}, f32[8,128]{1,0:T(8,128)}) custom-call(s32[2]{0:T(128)S(1)} %get-tuple-element.95.place_ref, f32[1280,1024]{1,0:T(8,128)} %get-tuple-element.126.refs_0_, bf16[1280,1024]{1,0:T(8,128)(2,1)} %collective-permute-done.27.refs_1_, ...), custom_call_target="tpu_custom_call", output_to_operand_aliasing={{0}: (3, {})} | custom-call | tf_op jit(solution)/shard_map/cond/branch_1_fun/final_rows/pallas_call | solution.py:62
  171.4 11.8 %collective-permute-done.26.refs_1_ = bf16[512,1024]{1,0:T(8,128)(2,1)} collective-permute-done((bf16[512,1024]{1,0:T(8,128)(2,1)}, bf16[512,1024]{1,0:T(8,128)(2,1)}, u32[]{:S(2)}, u32[]{:S(2)}) %collective-permute-start.26) | collective-permute-done | bytes 1048608 | tf_op jit(solution)/shard_map/cond/branch_1_fun/ppermute | solution.py:27
  183.2 4.5 %final_rows.17 = (f32[2048,1024]{1,0:T(8,128)}, f32[2048,1024]{1,0:T(8,128)}, f32[8,128]{1,0:T(8,128)}) custom-call(s32[2]{0:T(128)S(1)} %get-tuple-element.95.place_ref, f32[512,1024]{1,0:T(8,128)} %get-tuple-element.124.refs_0_, bf16[512,1024]{1,0:T(8,128)(2,1)} %collective-permute-done.26.refs_1_, ...), custom_call_target="tpu_custom_call", output_to_operand_aliasing={{0}: (3, {}), {1}: (5, {})} | custom-call | tf_op jit(solution)/shard_map/cond/branch_1_fun/final_rows/pallas_call | solution.py:62
  187.7 1.0 collective-permute-done.25.refs_1_
  188.7 0.7 copy-done.4
  189.4 2.9 %final_rows.18 = (f32[2048,1024]{1,0:T(8,128)}, f32[2048,1024]{1,0:T(8,128)}, f32[8,128]{1,0:T(8,128)}) custom-call(s32[2]{0:T(128)S(1)} %get-tuple-element.95.place_ref, f32[128,1024]{1,0:T(8,128)} %get-tuple-element.122.refs_0_, bf16[128,1024]{1,0:T(8,128)(2,1)} %copy-done.4, ...), custom_call_target="tpu_custom_call", output_to_operand_aliasing={{0}: (3, {}), {1}: (5, {})} | custom-call | tf_op jit(solution)/shard_map/cond/branch_1_fun/final_rows/pallas_call | solution.py:62
  192.3 1.2 collective-permute-done.24.refs_1_
  194.2 2.9 %final_rows.19 = (f32[2048,1024]{1,0:T(8,128)}, f32[2048,1024]{1,0:T(8,128)}, f32[8,128]{1,0:T(8,128)}) custom-call(s32[2]{0:T(128)S(1)} %get-tuple-element.95.place_ref, f32[128,1024]{1,0:T(8,128)} %get-tuple-element.120.refs_0_, bf16[128,1024]{1,0:T(8,128)(2,1)} %copy-done.1, ...), custom_call_target="tpu_custom_call", output_to_operand_aliasing={{0}: (3, {}), {1}: (5, {})} | custom-call | tf_op jit(solution)/shard_map/cond/branch_1_fun/final_rows/pallas_call | solution.py:62
  (23 shorter events, 2.5 us)
Async XLA Ops:
  1.6 11.3 %copy-start.7 = (s32[1,512]{1,0:T(1,128)S(1)}, s32[1,512]{1,0:T(1,128)}, u32[]{:S(2)}) copy-start(s32[1,512]{1,0:T(1,128)} %get-tuple-element.96.refs_0_) | copy-start | bytes 6148 | tf_op jit(solution)/shard_map/cond
  9.8 94.7 %collective-permute-start.18 = (bf16[2048,1024]{1,0:T(8,128)(2,1)}, bf16[2048,1024]{1,0:T(8,128)(2,1)}, u32[]{:S(2)}, u32[]{:S(2)}) collective-permute-start(bf16[2048,1024]{1,0:T(8,128)(2,1)} %get-tuple-element.101.refs_0_.refs_1_), channel_id=1, source_target_pairs={{0,8},{4,12},{8,0},{12,4},{16,24},{20,28},{24,16},{28,20},{1,9},{5... | collective-permute-start | bytes 12582920 | tf_op jit(solution)/shard_map/cond/branch_1_fun/ppermute | solution.py:27
  18.2 26.4 %collective-permute-start.19 = (bf16[512,1024]{1,0:T(8,128)(2,1)}, bf16[512,1024]{1,0:T(8,128)(2,1)}, u32[]{:S(2)}, u32[]{:S(2)}) collective-permute-start(bf16[512,1024]{1,0:T(8,128)(2,1)} %get-tuple-element.107), channel_id=1, source_target_pairs={{0,2},{2,0},{1,3},{3,1},{4,6},{6,4},{5,7},{7,5},{8,10},{10,8},{9,1... | collective-permute-start | bytes 3145736 | tf_op jit(solution)/shard_map/cond/branch_1_fun/ppermute | solution.py:22
  19.8 45.9 %collective-permute-start.16 = (bf16[512,1024]{1,0:T(8,128)(2,1)}, bf16[512,1024]{1,0:T(8,128)(2,1)}, u32[]{:S(2)}, u32[]{:S(2)}) collective-permute-start(bf16[512,1024]{1,0:T(8,128)(2,1)} %get-tuple-element.100.refs_2_.refs_0_), channel_id=1, source_target_pairs={{0,2},{2,0},{1,3},{3,1},{4,6},{6,4},{5,7},{7,5},{8,10},{10,8},{9,1... | collective-permute-start | bytes 3145736 | tf_op jit(solution)/shard_map/cond/branch_1_fun/ppermute | solution.py:22
  23.4 91.5 %collective-permute-start.15 = (bf16[1024,1024]{1,0:T(8,128)(2,1)}, bf16[1024,1024]{1,0:T(8,128)(2,1)}, u32[]{:S(2)}, u32[]{:S(2)}) collective-permute-start(bf16[1024,1024]{1,0:T(8,128)(2,1)} %get-tuple-element.105), channel_id=1, source_target_pairs={{0,1},{1,0},{2,3},{3,2},{4,5},{5,4},{6,7},{7,6},{8,9},{9,8},{10,11... | collective-permute-start | bytes 6291464 | tf_op jit(solution)/shard_map/cond/branch_1_fun/ppermute | solution.py:22
  44.6 21.0 %collective-permute-start.20 = (bf16[512,1024]{1,0:T(8,128)(2,1)}, bf16[512,1024]{1,0:T(8,128)(2,1)S(1)}, u32[]{:S(2)}, u32[]{:S(2)}) collective-permute-start(bf16[512,1024]{1,0:T(8,128)(2,1)} %collective-permute-done.19), channel_id=1, source_target_pairs={{0,1},{1,0},{2,3},{3,2},{4,5},{5,4},{6,7},{7,6},{8,9},{9,8},{10,11... | collective-permute-start | bytes 3145736 | tf_op jit(solution)/shard_map/cond/branch_1_fun/ppermute | solution.py:22
  65.6 49.3 %collective-permute-start.17 = (bf16[512,1024]{1,0:T(8,128)(2,1)}, bf16[512,1024]{1,0:T(8,128)(2,1)}, u32[]{:S(2)}, u32[]{:S(2)}) collective-permute-start(bf16[512,1024]{1,0:T(8,128)(2,1)} %collective-permute-done.16.refs_3_.refs_0_), channel_id=1, source_target_pairs={{0,1},{1,0},{2,3},{3,2},{4,5},{5,4},{6,7},{7,6},{8,9},{9,8},{10,11... | collective-permute-start | bytes 3145736 | tf_op jit(solution)/shard_map/cond/branch_1_fun/ppermute | solution.py:22
  80.4 80.3 %collective-permute-start.27 = (bf16[1280,1024]{1,0:T(8,128)(2,1)}, bf16[1280,1024]{1,0:T(8,128)(2,1)}, u32[]{:S(2)}, u32[]{:S(2)}) collective-permute-start(bf16[1280,1024]{1,0:T(8,128)(2,1)} %get-tuple-element.127), channel_id=1, source_target_pairs={{0,8},{4,12},{8,0},{12,4},{16,24},{20,28},{24,16},{28,20},{1,9},{5... | collective-permute-start | bytes 7864328 | tf_op jit(solution)/shard_map/cond/branch_1_fun/ppermute | solution.py:27
  80.7 43.0 %collective-permute-start.14 = (bf16[512,1024]{1,0:T(8,128)(2,1)}, bf16[512,1024]{1,0:T(8,128)(2,1)}, u32[]{:S(2)}, u32[]{:S(2)}) collective-permute-start(bf16[512,1024]{1,0:T(8,128)(2,1)} %get-tuple-element.100.refs_2_.refs_0_), channel_id=1, source_target_pairs={{0,1},{1,0},{2,3},{3,2},{4,5},{5,4},{6,7},{7,6},{8,9},{9,8},{10,11... | collective-permute-start | bytes 3145736 | tf_op jit(solution)/shard_map/cond/branch_1_fun/ppermute | solution.py:22
  121.7 23.8 %collective-permute-start.22 = (bf16[512,1024]{1,0:T(8,128)(2,1)}, bf16[512,1024]{1,0:T(8,128)(2,1)}, u32[]{:S(2)}, u32[]{:S(2)}) collective-permute-start(bf16[512,1024]{1,0:T(8,128)(2,1)} %get-tuple-element.117), channel_id=1, source_target_pairs={{0,2},{2,0},{1,3},{3,1},{4,6},{6,4},{5,7},{7,5},{8,10},{10,8},{9,1... | collective-permute-start | bytes 3145736 | tf_op jit(solution)/shard_map/cond/branch_1_fun/ppermute | solution.py:22
  123.7 23.9 %copy-start.10 = (bf16[128,1024]{1,0:T(8,128)(2,1)S(1)}, bf16[128,1024]{1,0:T(8,128)(2,1)}, u32[]{:S(2)}) copy-start(bf16[128,1024]{1,0:T(8,128)(2,1)} %get-tuple-element.121) | copy-start | bytes 786436 | tf_op jit(solution)/shard_map/cond
  130.6 17.0 %collective-permute-start.21 = (bf16[512,1024]{1,0:T(8,128)(2,1)}, bf16[512,1024]{1,0:T(8,128)(2,1)}, u32[]{:S(2)}, u32[]{:S(2)}) collective-permute-start(bf16[512,1024]{1,0:T(8,128)(2,1)} %get-tuple-element.116.refs_0_), channel_id=1, source_target_pairs={{0,1},{1,0},{2,3},{3,2},{4,5},{5,4},{6,7},{7,6},{8,9},{9,8},{10,11... | collective-permute-start | bytes 3145736 | tf_op jit(solution)/shard_map/cond/branch_1_fun/ppermute | solution.py:22
  145.6 3.5 %collective-permute-start.23 = (bf16[512,1024]{1,0:T(8,128)(2,1)}, bf16[512,1024]{1,0:T(8,128)(2,1)}, u32[]{:S(2)}, u32[]{:S(2)}) collective-permute-start(bf16[512,1024]{1,0:T(8,128)(2,1)} %collective-permute-done.22.refs_2_), channel_id=1, source_target_pairs={{0,1},{1,0},{2,3},{3,2},{4,5},{5,4},{6,7},{7,6},{8,9},{9,8},{10,11... | collective-permute-start | bytes 3145736 | tf_op jit(solution)/shard_map/cond/branch_1_fun/ppermute | solution.py:22
  145.6 37.7 %collective-permute-start.26 = (bf16[512,1024]{1,0:T(8,128)(2,1)}, bf16[512,1024]{1,0:T(8,128)(2,1)}, u32[]{:S(2)}, u32[]{:S(2)}) collective-permute-start(bf16[512,1024]{1,0:T(8,128)(2,1)} %get-tuple-element.125), channel_id=1, source_target_pairs={{0,8},{4,12},{8,0},{12,4},{16,24},{20,28},{24,16},{28,20},{1,9},{5... | collective-permute-start | bytes 3145736 | tf_op jit(solution)/shard_map/cond/branch_1_fun/ppermute | solution.py:27
  147.0 41.7 %collective-permute-start.25 = (bf16[128,1024]{1,0:T(8,128)(2,1)}, bf16[128,1024]{1,0:T(8,128)(2,1)S(1)}, u32[]{:S(2)}, u32[]{:S(2)}) collective-permute-start(bf16[128,1024]{1,0:T(8,128)(2,1)} %get-tuple-element.123), channel_id=1, source_target_pairs={{0,8},{4,12},{8,0},{12,4},{16,24},{20,28},{24,16},{28,20},{1,9},{5... | collective-permute-start | bytes 786440 | tf_op jit(solution)/shard_map/cond/branch_1_fun/ppermute | solution.py:27
  147.6 45.9 %collective-permute-start.24 = (bf16[128,1024]{1,0:T(8,128)(2,1)S(1)}, bf16[128,1024]{1,0:T(8,128)(2,1)S(1)}, u32[]{:S(2)}, u32[]{:S(2)}) collective-permute-start(bf16[128,1024]{1,0:T(8,128)(2,1)S(1)} %copy-done.10), channel_id=1, source_target_pairs={{0,8},{4,12},{8,0},{12,4},{16,24},{20,28},{24,16},{28,20},{1,9},{5... | collective-permute-start | bytes 786440 | tf_op jit(solution)/shard_map/cond/branch_1_fun/ppermute | solution.py:27
  188.7 0.7 copy-start.4
  193.5 0.7 copy-start.1

commit v2 on v1

--- a/solution.py
+++ b/solution.py
@@ -12,7 +12,8 @@
 warm_steps = 4096.0
 momentum_keep = 0.9
 
-velocity_parts = (10, 4, 1, 1)
+velocity_parts = (9, 5, 1, 1)
+weight_parts = (6, 10)
 
 any_spec = pl.BlockSpec(memory_space=pl.ANY)
 
@@ -46,8 +47,8 @@
 
 
 class Chain:
-    def __init__(self):
-        self.token = None
+    def __init__(self, token=None):
+        self.token = token
 
     def call(self, kernel, name, grid, places, ins, outs, aliases=()):
         ins = list(ins)
@@ -70,7 +71,7 @@
             out_shape=[jax.ShapeDtypeStruct(shape, kind) for shape, kind, _ in outs]
             + [jax.ShapeDtypeStruct((8, 128), jnp.float32)],
             input_output_aliases={i + 1: o for i, o in aliases},
-            compiler_params=pltpu.CompilerParams(vmem_limit_bytes=63 * 1024 * 1024),
+            compiler_params=pltpu.CompilerParams(vmem_limit_bytes=64 * 1024 * 1024 - 128 * 1024),
             cost_estimate=pl.CostEstimate(flops=0, bytes_accessed=0, transcendentals=0),
             name=name,
         )(places, *[array for array, _ in ins])
@@ -82,17 +83,19 @@
     outs[0][...] = ins[0][...].astype(outs[0].dtype)
 
 
-def cast_rows(chain, places, weight):
-    rows, cols = weight.shape
-    block = fitting(256, rows)
-    spec = pl.BlockSpec((block, cols), lambda r, at: (r, 0))
+def cast_rows(chain, places, weight, first, size):
+    cols = weight.shape[1]
+    block = fitting(512, first, size) if first else fitting(size, size)
+    if block > 512:
+        block = fitting(block // 2, size)
+    skip = first // block
     return chain.call(
         cast_kernel,
         "cast_rows",
-        (rows // block,),
-        places,
-        [(weight, spec)],
-        [((rows, cols), jnp.bfloat16, spec)],
+        (size // block,),
+        places,
+        [(weight, pl.BlockSpec((block, cols), lambda r, at: (skip + r, 0)))],
+        [((size, cols), jnp.bfloat16, pl.BlockSpec((block, cols), lambda r, at: (r, 0)))],
     )[0]
 
 
@@ -140,8 +143,8 @@
     )[0]
 
 
-def take_rows(chain, places, short):
-    half, cols = short.shape[0] // 2, short.shape[1]
+def take_rows(chain, places, weight):
+    half, cols = weight.shape[0] // 2, weight.shape[1]
     block = fitting(512, half)
     steps = half // block
     return chain.call(
@@ -149,8 +152,8 @@
         "take_rows",
         (steps,),
         places,
-        [(short, pl.BlockSpec((block, cols), lambda r, at: ((1 - at[1]) * steps + r, 0)))],
-        [((half, cols), short.dtype, pl.BlockSpec((block, cols), lambda r, at: (r, 0)))],
+        [(weight, pl.BlockSpec((block, cols), lambda r, at: ((1 - at[1]) * steps + r, 0)))],
+        [((half, cols), jnp.bfloat16, pl.BlockSpec((block, cols), lambda r, at: (r, 0)))],
     )[0]
 
 
@@ -189,14 +192,17 @@
 def input_kernel(places, ins, outs):
     own, other = (
         lax.dot_general(
-            ins[at][...], ins[at + 1][...], (((1,), (1,)), ((), ())), preferred_element_type=jnp.float32
+            ins[at][...],
+            ins[at + 1][...].astype(jnp.bfloat16),
+            (((1,), (1,)), ((), ())),
+            preferred_element_type=jnp.float32,
         )
         for at in (0, 2)
     )
     outs[0][...] = (own + other).astype(outs[0].dtype)
 
 
-def input_columns(chain, places, mask, short, mask_other, short_other):
+def input_columns(chain, places, mask, weight, mask_other, short_other):
     half, cols = short_other.shape
     toks = mask.shape[0]
     block = fitting(256, half)
@@ -209,7 +215,7 @@
         places,
         [
             (mask, mask_spec),
-            (short, pl.BlockSpec((block, cols), lambda r, at: (at[1] * steps + r, 0))),
+            (weight, pl.BlockSpec((block, cols), lambda r, at: (at[1] * steps + r, 0))),
             (mask_other, mask_spec),
             (short_other, pl.BlockSpec((block, cols), lambda r, at: (r, 0))),
         ],
@@ -250,17 +256,25 @@
     outs[0][...] = 0.5 * (ins[0][...] + ins[1][...].astype(jnp.float32))
 
 
-def half_rows(chain, places, weight, peer):
+def half_rows(chain, places, weight, peer, first, into):
     rows, cols = weight.shape
-    block = fitting(256, rows)
-    spec = pl.BlockSpec((block, cols), lambda r, at: (r, 0))
+    size = peer.shape[0]
+    block = fitting(512, first, size)
+    skip = first // block
+    whole_spec = pl.BlockSpec((block, cols), lambda r, at: (skip + r, 0))
+    ins = [(weight, whole_spec), (peer, pl.BlockSpec((block, cols), lambda r, at: (r, 0)))]
+    aliases = []
+    if into is not None:
+        aliases = [(len(ins), 0)]
+        ins.append((into, any_spec))
     return chain.call(
         half_kernel,
         "half_rows",
-        (rows // block,),
-        places,
-        [(weight, spec), (peer, spec)],
-        [((rows, cols), jnp.float32, spec)],
+        (size // block,),
+        places,
+        ins,
+        [((rows, cols), jnp.float32, whole_spec)],
+        aliases,
     )[0]
 
 
@@ -298,15 +312,17 @@
     )
 
 
-def step_with(bit, places, rate, ids, activation, cotangent, weight, momentum):
+def step_with(bit, token, first_short, places, rate, ids, activation, cotangent, weight, momentum):
     rows = weight.shape[0]
     n_dp = lax.axis_size("dp")
     mp = places[1]
     half = rows // 2
-    chain = Chain()
-
-    short = cast_rows(chain, places, weight)
-    weight_peer = from_partner(short, bit)
+    chain = Chain(token)
+
+    weight_pieces = starts_of(weight_parts, rows)
+    weight_peers = [from_partner(first_short, bit)]
+    for first, size in weight_pieces[1:]:
+        weight_peers.append(from_partner(cast_rows(chain, places, weight, first, size), bit))
 
     masked = mask_rows(chain, places, ids, cotangent)
     masks = [masked] + [shifted(masked, "dp", k) for k in range(1, n_dp)]
@@ -319,19 +335,21 @@
             jnp.where(mp == 0, jnp.concatenate([mine, other], 1), jnp.concatenate([other, mine], 1))
         )
 
-    short_other = shifted(take_rows(chain, places, short), "mp", 1)
+    new_weight = half_rows(chain, places, weight, weight_peers[0], 0, None)
+    short_other = shifted(take_rows(chain, places, weight), "mp", 1)
 
     velocities = []
     for first, size in starts_of(velocity_parts, rows):
         v, v_short = velocity_rows(chain, places, activation, others, masks, momentum, first, size)
         velocities.append((first, v, from_partner(v_short, bit)))
 
-    new_weight = half_rows(chain, places, weight, weight_peer)
+    for (first, _), peer in zip(weight_pieces[1:], weight_peers[1:]):
+        new_weight = half_rows(chain, places, weight, peer, first, new_weight)
 
     done = {}
     for k in reversed(range(n_dp)):
         done[k] = input_columns(
-            chain, places, masks[k], short, shifted(masks[k], "mp", 1), short_other
+            chain, places, masks[k], weight, shifted(masks[k], "mp", 1), short_other
         )
         if k:
             done[k] = shifted(done[k], "dp", n_dp - k)
@@ -353,9 +371,14 @@
     bit_count = lax.axis_size("outer").bit_length() - 1
     places = jnp.stack([lax.axis_index("dp"), lax.axis_index("mp")]).astype(jnp.int32)
     rate = (peak_rate * (step_index + 1).astype(jnp.float32) / warm_steps)[None]
+    chain = Chain()
+    first, size = starts_of(weight_parts, weight.shape[1])[0]
+    first_short = cast_rows(chain, places, weight[0], first, size)
     outs = lax.switch(
         step_index % bit_count,
         [functools.partial(step_with, bit) for bit in range(bit_count)],
+        chain.token,
+        first_short,
         places,
         rate,
         token_ids,

time: 198 us -> 193 us (0.975)
  waiting for transfers between devices: 88.5 us -> 71.2 us
  Pallas kernels: 90.8 us -> 103 us
    ppermute x9, waiting for transfers between devices: 57.2 us -> 28.6 us  [shifted(): return lax.ppermute(value, axis, [(s, (s + by) % n) for s in range(n)])]
    pallas_call x16 -> x18, Pallas kernels: 90.8 us -> 103 us  [call(): pl.pallas_call(body, grid_spec=pltpu.PrefetchScalarGridSpec(num_scalar_pr...]
    ppermute x5 -> x6, waiting for transfers between devices: 31.3 us -> 42.6 us  [from_partner(): return lax.ppermute(value, 'outer', [(s, s ^ 1 << bit) for s in range(n)])]
    ppermute x5 -> x6, starting transfers between devices: 6.76 us -> 7.31 us  [from_partner(): return lax.ppermute(value, 'outer', [(s, s ^ 1 << bit) for s in range(n)])]
  transfers between devices with their start and end apart: 14 -> 15, of which waited for: 8 -> 8; matrix products, arithmetic and copies ran while one was open for 2% -> 2% of each run, Pallas kernels for 40% -> 51%
where the time goes in v2:
time: 193 us; the launch traced here: 191 us
  Pallas kernels  103 us (53%)
  waiting for transfers between devices  71.2 us (37%)
  starting transfers between devices  11.7 us (6%)
  other arithmetic  3.8 us (2%)
    pallas_call x18, Pallas kernels, call(): pl.pallas_call(body, grid_spec=pltpu.PrefetchScalarGridSpec(num_scalar_pr...  103 us
    ppermute x6, waiting for transfers between devices, from_partner(): return lax.ppermute(value, 'outer', [(s, s ^ 1 << bit) for s in range(n)])  42.6 us
    ppermute x9, waiting for transfers between devices, shifted(): return lax.ppermute(value, axis, [(s, (s + by) % n) for s in range(n)])  28.6 us
    ppermute x6, starting transfers between devices, from_partner(): return lax.ppermute(value, 'outer', [(s, s ^ 1 << bit) for s in range(n)])  7.31 us
    ppermute x9, starting transfers between devices, shifted(): return lax.ppermute(value, axis, [(s, (s + by) % n) for s in range(n)])  4.37 us
  transfers between devices with their start and end apart: 15, of which 8 were waited for; matrix products, arithmetic and copies ran while one was open for 2% of the time, Pallas kernels for 51%

profile of v2, /device:TPU:0, one launch (start us, length us, event | category | flops | bytes accessed | tf_op | source)
XLA Modules:
  0.0 191.3 jit_solution(1927194227862256331)
XLA Ops:
  1.4 3.4 %cast_rows.7 = (bf16[768,1024]{1,0:T(8,128)(2,1)}, f32[8,128]{1,0:T(8,128)S(1)}) custom-call(s32[2]{0:T(128)S(1)} %pad_add_fusion.place_ref, f32[2048,1024]{1,0:T(8,128)} %bitcast.10), custom_call_target="tpu_custom_call" | custom-call | tf_op jit(solution)/shard_map/cast_rows/pallas_call | solution.py:63
  4.8 186.6 %conditional.1 = (bf16[512,4096]{1,0:T(8,128)(2,1)}, f32[2048,1024]{1,0:T(8,128)}, f32[2048,1024]{1,0:T(8,128)}) conditional(s32[]{:T(128)} %clamp.3, (s32[2]{0:T(128)S(1)}, f32[2048,1024]{1,0:T(8,128)}, f32[8,128]{1,0:T(8,128)S(1)}, s32[1,512]{1,0:T(1,128)S(1)}, bf16[512,1024]{1,0:T(8,128)(2,1)}, ...), branch_computations={%region_0.1_spmd, %region_1.2_spmd, %region_2.3_spmd} | conditional | flops 9437185 | bytes 79692408 | solution.py:377
  4.8 2.9 %collective-permute-start.1 = (bf16[768,1024]{1,0:T(8,128)(2,1)}, bf16[768,1024]{1,0:T(8,128)(2,1)}, u32[]{:S(2)}, u32[]{:S(2)}) collective-permute-start(bf16[768,1024]{1,0:T(8,128)(2,1)} %get-tuple-element.67), channel_id=1, source_target_pairs={{0,4},{4,0},{8,12},{12,8},{16,20},{20,16},{24,28},{28,24},{1,5},{5... | collective-permute-start | bytes 4718600 | tf_op jit(solution)/shard_map/cond/branch_0_fun/ppermute | solution.py:28
  7.7 6.1 %cast_rows.4 = (bf16[1280,1024]{1,0:T(8,128)(2,1)}, f32[8,128]{1,0:T(8,128)}) custom-call(s32[2]{0:T(128)S(1)} %get-tuple-element.60.place_ref, f32[2048,1024]{1,0:T(8,128)} %get-tuple-element.63.refs_0_.refs_1_, f32[8,128]{1,0:T(8,128)S(1)} %get-tuple-element.64.refs_1_), custom_call_target="tpu_custom_call" | custom-call | tf_op jit(solution)/shard_map/cond/branch_0_fun/cast_rows/pallas_call | solution.py:63
  13.8 2.8 %mask_rows.3 = (bf16[512,1024]{1,0:T(8,128)(2,1)}, f32[8,128]{1,0:T(8,128)}) custom-call(s32[2]{0:T(128)S(1)} %get-tuple-element.60.place_ref, s32[1,512]{1,0:T(1,128)S(1)} %get-tuple-element.61.refs_0_, bf16[512,1024]{1,0:T(8,128)(2,1)} %get-tuple-element.62.refs_1_, f32[8,128]{1,0:T(8,128)} %get-tuple-element.65.refs_2_), custom_call_target="tpu_custom_call" | custom-call | tf_op jit(solution)/shard_map/cond/branch_0_fun/mask_rows/pallas_call | solution.py:63
  16.6 2.6 %take_columns.3 = (bf16[512,1024]{1,0:T(8,128)(2,1)}, f32[8,128]{1,0:T(8,128)}) custom-call(s32[2]{0:T(128)S(1)} %get-tuple-element.60.place_ref, bf16[512,4096]{1,0:T(8,128)(2,1)} %get-tuple-element.68.refs_0_, f32[8,128]{1,0:T(8,128)} %get-tuple-element.69.refs_1_), custom_call_target="tpu_custom_call" | custom-call | tf_op jit(solution)/shard_map/cond/branch_0_fun/take_columns/pallas_call | solution.py:63
  19.2 1.5 collective-permute-start.6
  21.3 22.0 %collective-permute-done.1.refs_1_ = bf16[768,1024]{1,0:T(8,128)(2,1)} collective-permute-done((bf16[768,1024]{1,0:T(8,128)(2,1)}, bf16[768,1024]{1,0:T(8,128)(2,1)}, u32[]{:S(2)}, u32[]{:S(2)}) %collective-permute-start.1) | collective-permute-done | bytes 1572896 | tf_op jit(solution)/shard_map/cond/branch_0_fun/ppermute | solution.py:28
  43.3 5.3 %half_rows.6 = (f32[2048,1024]{1,0:T(8,128)}, f32[8,128]{1,0:T(8,128)}) custom-call(s32[2]{0:T(128)S(1)} %get-tuple-element.60.place_ref, f32[2048,1024]{1,0:T(8,128)} %get-tuple-element.63.refs_0_.refs_1_, bf16[768,1024]{1,0:T(8,128)(2,1)} %collective-permute-done.1.refs_1_, f32[8,128]{1,0:T(8,128)} %get-tuple-element.70.refs_2_), custom_call_target="tpu_custom_call" | custom-call | tf_op jit(solution)/shard_map/cond/branch_0_fun/half_rows/pallas_call | solution.py:63
  48.6 3.9 %take_rows.3 = (bf16[1024,1024]{1,0:T(8,128)(2,1)}, f32[8,128]{1,0:T(8,128)}) custom-call(s32[2]{0:T(128)S(1)} %get-tuple-element.60.place_ref, f32[2048,1024]{1,0:T(8,128)} %get-tuple-element.63.refs_0_.refs_1_, f32[8,128]{1,0:T(8,128)} %get-tuple-element.71.refs_1_), custom_call_target="tpu_custom_call" | custom-call | tf_op jit(solution)/shard_map/cond/branch_0_fun/take_rows/pallas_call | solution.py:63
  53.0 13.7 %collective-permute-done.3.refs_3_.refs_0_ = bf16[512,1024]{1,0:T(8,128)(2,1)} collective-permute-done((bf16[512,1024]{1,0:T(8,128)(2,1)}, bf16[512,1024]{1,0:T(8,128)(2,1)}, u32[]{:S(2)}, u32[]{:S(2)}) %collective-permute-start.3) | collective-permute-done | bytes 1048608 | tf_op jit(solution)/shard_map/cond/branch_0_fun/ppermute | solution.py:23
  66.6 3.7 %maximum_select_fusion.refs_1_ = bf16[512,2048]{1,0:T(8,128)(2,1)} fusion(bf16[512,1024]{1,0:T(8,128)(2,1)S(1)} %collective-permute-done.7, bf16[512,1024]{1,0:T(8,128)(2,1)} %collective-permute-done.6, pred[]{:T(512)S(6)} %eq.8), kind=kLoop, calls=%fused_computation | loop fusion | flops 9437184 | bytes 4194305 | tf_op jit(solution)/shard_map/cond/branch_0_fun/jit(_where)/select_n | solution.py:335
  70.3 12.2 %velocity_rows.12 = (f32[1152,1024]{1,0:T(8,128)}, bf16[1152,1024]{1,0:T(8,128)(2,1)}, f32[8,128]{1,0:T(8,128)}) custom-call(s32[2]{0:T(128)S(1)} %get-tuple-element.60.place_ref, bf16[512,4096]{1,0:T(8,128)(2,1)} %get-tuple-element.68.refs_0_, bf16[512,2048]{1,0:T(8,128)(2,1)} %maximum_select_fusion.refs_1_, ...), custom_call_target="tpu_custom_call" | custom-call | tf_op jit(solution)/shard_map/cond/branch_0_fun/velocity_rows/pallas_call | solution.py:63
  83.1 8.0 %velocity_rows.13 = (f32[640,1024]{1,0:T(8,128)}, bf16[640,1024]{1,0:T(8,128)(2,1)}, f32[8,128]{1,0:T(8,128)}) custom-call(s32[2]{0:T(128)S(1)} %get-tuple-element.60.place_ref, bf16[512,4096]{1,0:T(8,128)(2,1)} %get-tuple-element.68.refs_0_, bf16[512,2048]{1,0:T(8,128)(2,1)} %maximum_select_fusion.refs_1_, ...), custom_call_target="tpu_custom_call" | custom-call | tf_op jit(solution)/shard_map/cond/branch_0_fun/velocity_rows/pallas_call | solution.py:63
  91.1 3.7 %velocity_rows.14 = (f32[128,1024]{1,0:T(8,128)}, bf16[128,1024]{1,0:T(8,128)(2,1)}, f32[8,128]{1,0:T(8,128)}) custom-call(s32[2]{0:T(128)S(1)} %get-tuple-element.60.place_ref, bf16[512,4096]{1,0:T(8,128)(2,1)} %get-tuple-element.68.refs_0_, bf16[512,2048]{1,0:T(8,128)(2,1)} %maximum_select_fusion.refs_1_, ...), custom_call_target="tpu_custom_call" | custom-call | tf_op jit(solution)/shard_map/cond/branch_0_fun/velocity_rows/pallas_call | solution.py:63
  94.8 3.7 %velocity_rows.15 = (f32[128,1024]{1,0:T(8,128)}, bf16[128,1024]{1,0:T(8,128)(2,1)}, f32[8,128]{1,0:T(8,128)}) custom-call(s32[2]{0:T(128)S(1)} %get-tuple-element.60.place_ref, bf16[512,4096]{1,0:T(8,128)(2,1)} %get-tuple-element.68.refs_0_, bf16[512,2048]{1,0:T(8,128)(2,1)} %maximum_select_fusion.refs_1_, ...), custom_call_target="tpu_custom_call" | custom-call | tf_op jit(solution)/shard_map/cond/branch_0_fun/velocity_rows/pallas_call | solution.py:63
  98.5 0.9 collective-permute-done.5.refs_1_
  99.4 7.6 %half_rows.7 = (f32[2048,1024]{1,0:T(8,128)}, f32[8,128]{1,0:T(8,128)}) custom-call(s32[2]{0:T(128)S(1)} %get-tuple-element.60.place_ref, f32[2048,1024]{1,0:T(8,128)} %get-tuple-element.63.refs_0_.refs_1_, bf16[1280,1024]{1,0:T(8,128)(2,1)} %collective-permute-done.5.refs_1_, ...), custom_call_target="tpu_custom_call", output_to_operand_aliasing={{0}: (3, {})} | custom-call | tf_op jit(solution)/shard_map/cond/branch_0_fun/half_rows/pallas_call | solution.py:63
  107.1 7.2 %input_columns.6 = (bf16[512,1024]{1,0:T(8,128)(2,1)}, f32[8,128]{1,0:T(8,128)}) custom-call(s32[2]{0:T(128)S(1)} %get-tuple-element.60.place_ref, bf16[512,1024]{1,0:T(8,128)(2,1)} %collective-permute-done.3.refs_3_.refs_0_, f32[2048,1024]{1,0:T(8,128)} %get-tuple-element.63.refs_0_.refs_1_, bf16[512,1024]{1,0:T(8,128)(2,1)} %collective-permute-done.4.refs_2_, ...), custom_call_target="tpu_custom_call" | custom-call | tf_op jit(solution)/shard_map/cond/branch_0_fun/input_columns/pallas_call | solution.py:63
  114.2 2.1 %collective-permute-start.9 = (bf16[512,1024]{1,0:T(8,128)(2,1)}, bf16[512,1024]{1,0:T(8,128)(2,1)}, u32[]{:S(2)}, u32[]{:S(2)}) collective-permute-start(bf16[512,1024]{1,0:T(8,128)(2,1)} %get-tuple-element.86), channel_id=1, source_target_pairs={{0,2},{2,0},{1,3},{3,1},{4,6},{6,4},{5,7},{7,5},{8,10},{10,8},{9,1... | collective-permute-start | bytes 3145736 | tf_op jit(solution)/shard_map/cond/branch_0_fun/ppermute | solution.py:23
  116.3 1.5 collective-permute-start.13
  117.8 7.2 %input_columns.7 = (bf16[512,1024]{1,0:T(8,128)(2,1)}, f32[8,128]{1,0:T(8,128)}) custom-call(s32[2]{0:T(128)S(1)} %get-tuple-element.60.place_ref, bf16[512,1024]{1,0:T(8,128)(2,1)} %get-tuple-element.66.refs_2_.refs_0_, f32[2048,1024]{1,0:T(8,128)} %get-tuple-element.63.refs_0_.refs_1_, bf16[512,1024]{1,0:T(8,128)(2,1)} %collective-permute-done.refs_2_, ...), custom_call_target="tpu_custom_call" | custom-call | tf_op jit(solution)/shard_map/cond/branch_0_fun/input_columns/pallas_call | solution.py:63
  125.0 14.0 %collective-permute-done.9.refs_2_ = bf16[512,1024]{1,0:T(8,128)(2,1)} collective-permute-done((bf16[512,1024]{1,0:T(8,128)(2,1)}, bf16[512,1024]{1,0:T(8,128)(2,1)}, u32[]{:S(2)}, u32[]{:S(2)}) %collective-permute-start.9) | collective-permute-done | bytes 1048608 | tf_op jit(solution)/shard_map/cond/branch_0_fun/ppermute | solution.py:23
  138.9 1.7 collective-permute-start.12
  141.0 1.0 collective-permute-done.10.refs_3_
  141.9 5.2 %join_columns.3 = (bf16[512,4096]{1,0:T(8,128)(2,1)}, f32[8,128]{1,0:T(8,128)}) custom-call(s32[2]{0:T(128)S(1)} %get-tuple-element.60.place_ref, bf16[512,1024]{1,0:T(8,128)(2,1)} %get-tuple-element.85.refs_0_, bf16[512,1024]{1,0:T(8,128)(2,1)} %collective-permute-done.8.refs_1_, bf16[512,1024]{1,0:T(8,128)(2,1)} %collective-permute-done.9.refs_2_, ...), custom_call_target="tpu_custom_call" | custom-call | tf_op jit(solution)/shard_map/cond/branch_0_fun/join_columns/pallas_call | solution.py:63
  147.1 2.9 %collective-permute-done.14.refs_1_ = bf16[1152,1024]{1,0:T(8,128)(2,1)} collective-permute-done((bf16[1152,1024]{1,0:T(8,128)(2,1)}, bf16[1152,1024]{1,0:T(8,128)(2,1)}, u32[]{:S(2)}, u32[]{:S(2)}) %collective-permute-start.14) | collective-permute-done | bytes 2359328 | tf_op jit(solution)/shard_map/cond/branch_0_fun/ppermute | solution.py:28
  150.0 11.6 %final_rows.12 = (f32[2048,1024]{1,0:T(8,128)}, f32[2048,1024]{1,0:T(8,128)}, f32[8,128]{1,0:T(8,128)}) custom-call(s32[2]{0:T(128)S(1)} %get-tuple-element.60.place_ref, f32[1152,1024]{1,0:T(8,128)} %get-tuple-element.95.refs_0_, bf16[1152,1024]{1,0:T(8,128)(2,1)} %collective-permute-done.14.refs_1_, ...), custom_call_target="tpu_custom_call", output_to_operand_aliasing={{0}: (3, {})} | custom-call | tf_op jit(solution)/shard_map/cond/branch_0_fun/final_rows/pallas_call | solution.py:63
  161.6 16.5 %collective-permute-done.13.refs_1_ = bf16[640,1024]{1,0:T(8,128)(2,1)} collective-permute-done((bf16[640,1024]{1,0:T(8,128)(2,1)}, bf16[640,1024]{1,0:T(8,128)(2,1)}, u32[]{:S(2)}, u32[]{:S(2)}) %collective-permute-start.13) | collective-permute-done | bytes 1310752 | tf_op jit(solution)/shard_map/cond/branch_0_fun/ppermute | solution.py:28
  178.1 7.2 %final_rows.13 = (f32[2048,1024]{1,0:T(8,128)}, f32[2048,1024]{1,0:T(8,128)}, f32[8,128]{1,0:T(8,128)}) custom-call(s32[2]{0:T(128)S(1)} %get-tuple-element.60.place_ref, f32[640,1024]{1,0:T(8,128)} %get-tuple-element.93.refs_0_, bf16[640,1024]{1,0:T(8,128)(2,1)} %collective-permute-done.13.refs_1_, ...), custom_call_target="tpu_custom_call", output_to_operand_aliasing={{0}: (3, {}), {1}: (5, {})} | custom-call | tf_op jit(solution)/shard_map/cond/branch_0_fun/final_rows/pallas_call | solution.py:63
  185.3 2.9 %final_rows.14 = (f32[2048,1024]{1,0:T(8,128)}, f32[2048,1024]{1,0:T(8,128)}, f32[8,128]{1,0:T(8,128)}) custom-call(s32[2]{0:T(128)S(1)} %get-tuple-element.60.place_ref, f32[128,1024]{1,0:T(8,128)} %get-tuple-element.91.refs_0_, bf16[128,1024]{1,0:T(8,128)(2,1)} %collective-permute-done.12.refs_1_, ...), custom_call_target="tpu_custom_call", output_to_operand_aliasing={{0}: (3, {}), {1}: (5, {})} | custom-call | tf_op jit(solution)/shard_map/cond/branch_0_fun/final_rows/pallas_call | solution.py:63
  188.5 2.9 %final_rows.15 = (f32[2048,1024]{1,0:T(8,128)}, f32[2048,1024]{1,0:T(8,128)}, f32[8,128]{1,0:T(8,128)}) custom-call(s32[2]{0:T(128)S(1)} %get-tuple-element.60.place_ref, f32[128,1024]{1,0:T(8,128)} %get-tuple-element.89.refs_0_, bf16[128,1024]{1,0:T(8,128)(2,1)} %collective-permute-done.11.refs_1_, ...), custom_call_target="tpu_custom_call", output_to_operand_aliasing={{0}: (3, {}), {1}: (5, {})} | custom-call | tf_op jit(solution)/shard_map/cond/branch_0_fun/final_rows/pallas_call | solution.py:63
  (21 shorter events, 2.3 us)
Async XLA Ops:
  1.4 3.4 %copy-start = (s32[1,512]{1,0:T(1,128)S(1)}, s32[1,512]{1,0:T(1,128)}, u32[]{:S(2)}) copy-start(s32[1,512]{1,0:T(1,128)} %param.10) | copy-start | bytes 6148
  4.8 38.5 %collective-permute-start.1 = (bf16[768,1024]{1,0:T(8,128)(2,1)}, bf16[768,1024]{1,0:T(8,128)(2,1)}, u32[]{:S(2)}, u32[]{:S(2)}) collective-permute-start(bf16[768,1024]{1,0:T(8,128)(2,1)} %get-tuple-element.67), channel_id=1, source_target_pairs={{0,4},{4,0},{8,12},{12,8},{16,20},{20,16},{24,28},{28,24},{1,5},{5... | collective-permute-start | bytes 4718600 | tf_op jit(solution)/shard_map/cond/branch_0_fun/ppermute | solution.py:28
  19.2 33.2 %collective-permute-start.6 = (bf16[512,1024]{1,0:T(8,128)(2,1)}, bf16[512,1024]{1,0:T(8,128)(2,1)}, u32[]{:S(2)}, u32[]{:S(2)}) collective-permute-start(bf16[512,1024]{1,0:T(8,128)(2,1)} %get-tuple-element.76), channel_id=1, source_target_pairs={{0,2},{2,0},{1,3},{3,1},{4,6},{6,4},{5,7},{7,5},{8,10},{10,8},{9,1... | collective-permute-start | bytes 3145736 | tf_op jit(solution)/shard_map/cond/branch_0_fun/ppermute | solution.py:23
  20.7 78.7 %collective-permute-start.5 = (bf16[1280,1024]{1,0:T(8,128)(2,1)}, bf16[1280,1024]{1,0:T(8,128)(2,1)}, u32[]{:S(2)}, u32[]{:S(2)}) collective-permute-start(bf16[1280,1024]{1,0:T(8,128)(2,1)} %get-tuple-element.73), channel_id=1, source_target_pairs={{0,4},{4,0},{8,12},{12,8},{16,20},{20,16},{24,28},{28,24},{1,5},{5... | collective-permute-start | bytes 7864328 | tf_op jit(solution)/shard_map/cond/branch_0_fun/ppermute | solution.py:28
  21.3 45.4 %collective-permute-start.3 = (bf16[512,1024]{1,0:T(8,128)(2,1)}, bf16[512,1024]{1,0:T(8,128)(2,1)}, u32[]{:S(2)}, u32[]{:S(2)}) collective-permute-start(bf16[512,1024]{1,0:T(8,128)(2,1)} %get-tuple-element.66.refs_2_.refs_0_), channel_id=1, source_target_pairs={{0,2},{2,0},{1,3},{3,1},{4,6},{6,4},{5,7},{7,5},{8,10},{10,8},{9,1... | collective-permute-start | bytes 3145736 | tf_op jit(solution)/shard_map/cond/branch_0_fun/ppermute | solution.py:23
  52.4 54.6 %collective-permute-start.2 = (bf16[1024,1024]{1,0:T(8,128)(2,1)}, bf16[1024,1024]{1,0:T(8,128)(2,1)}, u32[]{:S(2)}, u32[]{:S(2)}) collective-permute-start(bf16[1024,1024]{1,0:T(8,128)(2,1)} %get-tuple-element.72), channel_id=1, source_target_pairs={{0,1},{1,0},{2,3},{3,2},{4,5},{5,4},{6,7},{7,6},{8,9},{9,8},{10,11... | collective-permute-start | bytes 6291464 | tf_op jit(solution)/shard_map/cond/branch_0_fun/ppermute | solution.py:23
  52.4 14.2 %collective-permute-start.7 = (bf16[512,1024]{1,0:T(8,128)(2,1)}, bf16[512,1024]{1,0:T(8,128)(2,1)S(1)}, u32[]{:S(2)}, u32[]{:S(2)}) collective-permute-start(bf16[512,1024]{1,0:T(8,128)(2,1)} %collective-permute-done.6), channel_id=1, source_target_pairs={{0,1},{1,0},{2,3},{3,2},{4,5},{5,4},{6,7},{7,6},{8,9},{9,8},{10,11... | collective-permute-start | bytes 3145736 | tf_op jit(solution)/shard_map/cond/branch_0_fun/ppermute | solution.py:23
  66.6 40.5 %collective-permute-start.4 = (bf16[512,1024]{1,0:T(8,128)(2,1)}, bf16[512,1024]{1,0:T(8,128)(2,1)}, u32[]{:S(2)}, u32[]{:S(2)}) collective-permute-start(bf16[512,1024]{1,0:T(8,128)(2,1)} %collective-permute-done.3.refs_3_.refs_0_), channel_id=1, source_target_pairs={{0,1},{1,0},{2,3},{3,2},{4,5},{5,4},{6,7},{7,6},{8,9},{9,8},{10,11... | collective-permute-start | bytes 3145736 | tf_op jit(solution)/shard_map/cond/branch_0_fun/ppermute | solution.py:23
  82.5 67.5 %collective-permute-start.14 = (bf16[1152,1024]{1,0:T(8,128)(2,1)}, bf16[1152,1024]{1,0:T(8,128)(2,1)}, u32[]{:S(2)}, u32[]{:S(2)}) collective-permute-start(bf16[1152,1024]{1,0:T(8,128)(2,1)} %get-tuple-element.96), channel_id=1, source_target_pairs={{0,4},{4,0},{8,12},{12,8},{16,20},{20,16},{24,28},{28,24},{1,5},{5... | collective-permute-start | bytes 7077896 | tf_op jit(solution)/shard_map/cond/branch_0_fun/ppermute | solution.py:28
  82.8 35.0 %collective-permute-start = (bf16[512,1024]{1,0:T(8,128)(2,1)}, bf16[512,1024]{1,0:T(8,128)(2,1)}, u32[]{:S(2)}, u32[]{:S(2)}) collective-permute-start(bf16[512,1024]{1,0:T(8,128)(2,1)} %get-tuple-element.66.refs_2_.refs_0_), channel_id=1, source_target_pairs={{0,1},{1,0},{2,3},{3,2},{4,5},{5,4},{6,7},{7,6},{8,9},{9,8},{10,11... | collective-permute-start | bytes 3145736 | tf_op jit(solution)/shard_map/cond/branch_0_fun/ppermute | solution.py:23
  114.2 24.7 %collective-permute-start.9 = (bf16[512,1024]{1,0:T(8,128)(2,1)}, bf16[512,1024]{1,0:T(8,128)(2,1)}, u32[]{:S(2)}, u32[]{:S(2)}) collective-permute-start(bf16[512,1024]{1,0:T(8,128)(2,1)} %get-tuple-element.86), channel_id=1, source_target_pairs={{0,2},{2,0},{1,3},{3,1},{4,6},{6,4},{5,7},{7,5},{8,10},{10,8},{9,1... | collective-permute-start | bytes 3145736 | tf_op jit(solution)/shard_map/cond/branch_0_fun/ppermute | solution.py:23
  116.3 61.8 %collective-permute-start.13 = (bf16[640,1024]{1,0:T(8,128)(2,1)}, bf16[640,1024]{1,0:T(8,128)(2,1)}, u32[]{:S(2)}, u32[]{:S(2)}) collective-permute-start(bf16[640,1024]{1,0:T(8,128)(2,1)} %get-tuple-element.94), channel_id=1, source_target_pairs={{0,4},{4,0},{8,12},{12,8},{16,20},{20,16},{24,28},{28,24},{1,5},{5... | collective-permute-start | bytes 3932168 | tf_op jit(solution)/shard_map/cond/branch_0_fun/ppermute | solution.py:28
  125.0 15.7 %collective-permute-start.8 = (bf16[512,1024]{1,0:T(8,128)(2,1)}, bf16[512,1024]{1,0:T(8,128)(2,1)}, u32[]{:S(2)}, u32[]{:S(2)}) collective-permute-start(bf16[512,1024]{1,0:T(8,128)(2,1)} %get-tuple-element.85.refs_0_), channel_id=1, source_target_pairs={{0,1},{1,0},{2,3},{3,2},{4,5},{5,4},{6,7},{7,6},{8,9},{9,8},{10,11... | collective-permute-start | bytes 3145736 | tf_op jit(solution)/shard_map/cond/branch_0_fun/ppermute | solution.py:23
  138.9 3.0 %collective-permute-start.10 = (bf16[512,1024]{1,0:T(8,128)(2,1)}, bf16[512,1024]{1,0:T(8,128)(2,1)}, u32[]{:S(2)}, u32[]{:S(2)}) collective-permute-start(bf16[512,1024]{1,0:T(8,128)(2,1)} %collective-permute-done.9.refs_2_), channel_id=1, source_target_pairs={{0,1},{1,0},{2,3},{3,2},{4,5},{5,4},{6,7},{7,6},{8,9},{9,8},{10,11... | collective-permute-start | bytes 3145736 | tf_op jit(solution)/shard_map/cond/branch_0_fun/ppermute | solution.py:23
  138.9 46.4 %collective-permute-start.12 = (bf16[128,1024]{1,0:T(8,128)(2,1)}, bf16[128,1024]{1,0:T(8,128)(2,1)}, u32[]{:S(2)}, u32[]{:S(2)}) collective-permute-start(bf16[128,1024]{1,0:T(8,128)(2,1)} %get-tuple-element.92), channel_id=1, source_target_pairs={{0,4},{4,0},{8,12},{12,8},{16,20},{20,16},{24,28},{28,24},{1,5},{5... | collective-permute-start | bytes 786440 | tf_op jit(solution)/shard_map/cond/branch_0_fun/ppermute | solution.py:28
  140.7 47.8 %collective-permute-start.11 = (bf16[128,1024]{1,0:T(8,128)(2,1)}, bf16[128,1024]{1,0:T(8,128)(2,1)}, u32[]{:S(2)}, u32[]{:S(2)}) collective-permute-start(bf16[128,1024]{1,0:T(8,128)(2,1)} %get-tuple-element.90), channel_id=1, source_target_pairs={{0,4},{4,0},{8,12},{12,8},{16,20},{20,16},{24,28},{28,24},{1,5},{5... | collective-permute-start | bytes 786440 | tf_op jit(solution)/shard_map/cond/branch_0_fun/ppermute | solution.py:28

commit v3 on v2

--- a/solution.py
+++ b/solution.py
@@ -44,6 +44,15 @@
     while any(size % block for size in sizes):
         block //= 2
     return block
+
+
+def by_slabs(ref, body):
+    rows = ref.shape[0]
+    slab = fitting(64, rows)
+
+    @pl.loop(0, rows // slab)
+    def _(step):
+        body(pl.ds(pl.multiple_of(step * slab, slab), slab))
 
 
 class Chain:
@@ -80,7 +89,10 @@
 
 
 def cast_kernel(places, ins, outs):
-    outs[0][...] = ins[0][...].astype(outs[0].dtype)
+    def slab(at):
+        outs[0][at] = ins[0][at].astype(outs[0].dtype)
+
+    by_slabs(outs[0], slab)
 
 
 def cast_rows(chain, places, weight, first, size):
@@ -231,7 +243,11 @@
 
         @pl.when(piece == at)
         def _():
-            outs[0][...] = ins[at][...]
+
+            def slab(rows):
+                outs[0][rows] = ins[at][rows]
+
+            by_slabs(outs[0], slab)
 
 
 def join_columns(chain, places, pieces):
@@ -253,7 +269,10 @@
 
 
 def half_kernel(places, ins, outs):
-    outs[0][...] = 0.5 * (ins[0][...] + ins[1][...].astype(jnp.float32))
+    def slab(at):
+        outs[0][at] = 0.5 * (ins[0][at] + ins[1][at].astype(jnp.float32))
+
+    by_slabs(outs[0], slab)
 
 
 def half_rows(chain, places, weight, peer, first, into):
@@ -279,9 +298,12 @@
 
 
 def final_kernel(places, ins, outs):
-    mean = 0.5 * (ins[0][...] + ins[1][...].astype(jnp.float32))
-    outs[1][...] = mean
-    outs[0][...] = ins[2][...] - ins[3][0] * mean
+    def slab(at):
+        mean = 0.5 * (ins[0][at] + ins[1][at].astype(jnp.float32))
+        outs[1][at] = mean
+        outs[0][at] = ins[2][at] - ins[3][0] * mean
+
+    by_slabs(outs[0], slab)
 
 
 def final_rows(chain, places, rate, v, peer, half, into, first):

time: 193 us -> 193 us (level)
  no operation moved by 1% of the time
where the time goes in v3:
time: 193 us; the launch traced here: 191 us
  Pallas kernels  104 us (54%)
  waiting for transfers between devices  70.7 us (37%)
  starting transfers between devices  11.7 us (6%)
  other arithmetic  3.8 us (2%)
    pallas_call x18, Pallas kernels, call(): pl.pallas_call(body, grid_spec=pltpu.PrefetchScalarGridSpec(num_scalar_pr...  104 us
    ppermute x6, waiting for transfers between devices, from_partner(): return lax.ppermute(value, 'outer', [(s, s ^ 1 << bit) for s in range(n)])  42.1 us
    ppermute x9, waiting for transfers between devices, shifted(): return lax.ppermute(value, axis, [(s, (s + by) % n) for s in range(n)])  28.6 us
    ppermute x6, starting transfers between devices, from_partner(): return lax.ppermute(value, 'outer', [(s, s ^ 1 << bit) for s in range(n)])  7.3 us
    ppermute x9, starting transfers between devices, shifted(): return lax.ppermute(value, axis, [(s, (s + by) % n) for s in range(n)])  4.4 us
  transfers between devices with their start and end apart: 15, of which 8 were waited for; matrix products, arithmetic and copies ran while one was open for 2% of the time, Pallas kernels for 51%

profile of v3, /device:TPU:0, one launch (start us, length us, event | category | flops | bytes accessed | tf_op | source)
XLA Modules:
  0.0 191.4 jit_solution(6496327965777446704)
XLA Ops:
  1.4 3.4 %cast_rows.7 = (bf16[768,1024]{1,0:T(8,128)(2,1)}, f32[8,128]{1,0:T(8,128)S(1)}) custom-call(s32[2]{0:T(128)S(1)} %pad_add_fusion.place_ref, f32[2048,1024]{1,0:T(8,128)} %bitcast.10), custom_call_target="tpu_custom_call" | custom-call | tf_op jit(solution)/shard_map/cast_rows/pallas_call | solution.py:72
  4.8 186.6 %conditional.1 = (bf16[512,4096]{1,0:T(8,128)(2,1)}, f32[2048,1024]{1,0:T(8,128)}, f32[2048,1024]{1,0:T(8,128)}) conditional(s32[]{:T(128)} %clamp.3, (s32[2]{0:T(128)S(1)}, f32[2048,1024]{1,0:T(8,128)}, f32[8,128]{1,0:T(8,128)S(1)}, s32[1,512]{1,0:T(1,128)S(1)}, bf16[512,1024]{1,0:T(8,128)(2,1)}, ...), branch_computations={%region_0.1_spmd, %region_1.2_spmd, %region_2.3_spmd} | conditional | flops 9437185 | bytes 79692408 | solution.py:399
  4.8 2.9 %collective-permute-start.1 = (bf16[768,1024]{1,0:T(8,128)(2,1)}, bf16[768,1024]{1,0:T(8,128)(2,1)}, u32[]{:S(2)}, u32[]{:S(2)}) collective-permute-start(bf16[768,1024]{1,0:T(8,128)(2,1)} %get-tuple-element.67), channel_id=1, source_target_pairs={{0,4},{4,0},{8,12},{12,8},{16,20},{20,16},{24,28},{28,24},{1,5},{5... | collective-permute-start | bytes 4718600 | tf_op jit(solution)/shard_map/cond/branch_0_fun/ppermute | solution.py:28
  7.7 6.1 %cast_rows.4 = (bf16[1280,1024]{1,0:T(8,128)(2,1)}, f32[8,128]{1,0:T(8,128)}) custom-call(s32[2]{0:T(128)S(1)} %get-tuple-element.60.place_ref, f32[2048,1024]{1,0:T(8,128)} %get-tuple-element.63.refs_0_.refs_1_, f32[8,128]{1,0:T(8,128)S(1)} %get-tuple-element.64.refs_1_), custom_call_target="tpu_custom_call" | custom-call | tf_op jit(solution)/shard_map/cond/branch_0_fun/cast_rows/pallas_call | solution.py:72
  13.9 2.8 %mask_rows.3 = (bf16[512,1024]{1,0:T(8,128)(2,1)}, f32[8,128]{1,0:T(8,128)}) custom-call(s32[2]{0:T(128)S(1)} %get-tuple-element.60.place_ref, s32[1,512]{1,0:T(1,128)S(1)} %get-tuple-element.61.refs_0_, bf16[512,1024]{1,0:T(8,128)(2,1)} %get-tuple-element.62.refs_1_, f32[8,128]{1,0:T(8,128)} %get-tuple-element.65.refs_2_), custom_call_target="tpu_custom_call" | custom-call | tf_op jit(solution)/shard_map/cond/branch_0_fun/mask_rows/pallas_call | solution.py:72
  16.6 2.6 %take_columns.3 = (bf16[512,1024]{1,0:T(8,128)(2,1)}, f32[8,128]{1,0:T(8,128)}) custom-call(s32[2]{0:T(128)S(1)} %get-tuple-element.60.place_ref, bf16[512,4096]{1,0:T(8,128)(2,1)} %get-tuple-element.68.refs_0_, f32[8,128]{1,0:T(8,128)} %get-tuple-element.69.refs_1_), custom_call_target="tpu_custom_call" | custom-call | tf_op jit(solution)/shard_map/cond/branch_0_fun/take_columns/pallas_call | solution.py:72
  19.2 1.5 collective-permute-start.6
  21.3 22.0 %collective-permute-done.1.refs_1_ = bf16[768,1024]{1,0:T(8,128)(2,1)} collective-permute-done((bf16[768,1024]{1,0:T(8,128)(2,1)}, bf16[768,1024]{1,0:T(8,128)(2,1)}, u32[]{:S(2)}, u32[]{:S(2)}) %collective-permute-start.1) | collective-permute-done | bytes 1572896 | tf_op jit(solution)/shard_map/cond/branch_0_fun/ppermute | solution.py:28
  43.3 5.3 %half_rows.6 = (f32[2048,1024]{1,0:T(8,128)}, f32[8,128]{1,0:T(8,128)}) custom-call(s32[2]{0:T(128)S(1)} %get-tuple-element.60.place_ref, f32[2048,1024]{1,0:T(8,128)} %get-tuple-element.63.refs_0_.refs_1_, bf16[768,1024]{1,0:T(8,128)(2,1)} %collective-permute-done.1.refs_1_, f32[8,128]{1,0:T(8,128)} %get-tuple-element.70.refs_2_), custom_call_target="tpu_custom_call" | custom-call | tf_op jit(solution)/shard_map/cond/branch_0_fun/half_rows/pallas_call | solution.py:72
  48.6 3.9 %take_rows.3 = (bf16[1024,1024]{1,0:T(8,128)(2,1)}, f32[8,128]{1,0:T(8,128)}) custom-call(s32[2]{0:T(128)S(1)} %get-tuple-element.60.place_ref, f32[2048,1024]{1,0:T(8,128)} %get-tuple-element.63.refs_0_.refs_1_, f32[8,128]{1,0:T(8,128)} %get-tuple-element.71.refs_1_), custom_call_target="tpu_custom_call" | custom-call | tf_op jit(solution)/shard_map/cond/branch_0_fun/take_rows/pallas_call | solution.py:72
  53.0 13.6 %collective-permute-done.3.refs_3_.refs_0_ = bf16[512,1024]{1,0:T(8,128)(2,1)} collective-permute-done((bf16[512,1024]{1,0:T(8,128)(2,1)}, bf16[512,1024]{1,0:T(8,128)(2,1)}, u32[]{:S(2)}, u32[]{:S(2)}) %collective-permute-start.3) | collective-permute-done | bytes 1048608 | tf_op jit(solution)/shard_map/cond/branch_0_fun/ppermute | solution.py:23
  66.7 3.7 %maximum_select_fusion.refs_1_ = bf16[512,2048]{1,0:T(8,128)(2,1)} fusion(bf16[512,1024]{1,0:T(8,128)(2,1)S(1)} %collective-permute-done.7, bf16[512,1024]{1,0:T(8,128)(2,1)} %collective-permute-done.6, pred[]{:T(512)S(6)} %eq.8), kind=kLoop, calls=%fused_computation | loop fusion | flops 9437184 | bytes 4194305 | tf_op jit(solution)/shard_map/cond/branch_0_fun/jit(_where)/select_n | solution.py:357
  70.4 12.2 %velocity_rows.12 = (f32[1152,1024]{1,0:T(8,128)}, bf16[1152,1024]{1,0:T(8,128)(2,1)}, f32[8,128]{1,0:T(8,128)}) custom-call(s32[2]{0:T(128)S(1)} %get-tuple-element.60.place_ref, bf16[512,4096]{1,0:T(8,128)(2,1)} %get-tuple-element.68.refs_0_, bf16[512,2048]{1,0:T(8,128)(2,1)} %maximum_select_fusion.refs_1_, ...), custom_call_target="tpu_custom_call" | custom-call | tf_op jit(solution)/shard_map/cond/branch_0_fun/velocity_rows/pallas_call | solution.py:72
  83.1 8.0 %velocity_rows.13 = (f32[640,1024]{1,0:T(8,128)}, bf16[640,1024]{1,0:T(8,128)(2,1)}, f32[8,128]{1,0:T(8,128)}) custom-call(s32[2]{0:T(128)S(1)} %get-tuple-element.60.place_ref, bf16[512,4096]{1,0:T(8,128)(2,1)} %get-tuple-element.68.refs_0_, bf16[512,2048]{1,0:T(8,128)(2,1)} %maximum_select_fusion.refs_1_, ...), custom_call_target="tpu_custom_call" | custom-call | tf_op jit(solution)/shard_map/cond/branch_0_fun/velocity_rows/pallas_call | solution.py:72
  91.1 3.7 %velocity_rows.14 = (f32[128,1024]{1,0:T(8,128)}, bf16[128,1024]{1,0:T(8,128)(2,1)}, f32[8,128]{1,0:T(8,128)}) custom-call(s32[2]{0:T(128)S(1)} %get-tuple-element.60.place_ref, bf16[512,4096]{1,0:T(8,128)(2,1)} %get-tuple-element.68.refs_0_, bf16[512,2048]{1,0:T(8,128)(2,1)} %maximum_select_fusion.refs_1_, ...), custom_call_target="tpu_custom_call" | custom-call | tf_op jit(solution)/shard_map/cond/branch_0_fun/velocity_rows/pallas_call | solution.py:72
  94.8 3.7 %velocity_rows.15 = (f32[128,1024]{1,0:T(8,128)}, bf16[128,1024]{1,0:T(8,128)(2,1)}, f32[8,128]{1,0:T(8,128)}) custom-call(s32[2]{0:T(128)S(1)} %get-tuple-element.60.place_ref, bf16[512,4096]{1,0:T(8,128)(2,1)} %get-tuple-element.68.refs_0_, bf16[512,2048]{1,0:T(8,128)(2,1)} %maximum_select_fusion.refs_1_, ...), custom_call_target="tpu_custom_call" | custom-call | tf_op jit(solution)/shard_map/cond/branch_0_fun/velocity_rows/pallas_call | solution.py:72
  98.6 0.9 collective-permute-done.5.refs_1_
  99.5 7.6 %half_rows.7 = (f32[2048,1024]{1,0:T(8,128)}, f32[8,128]{1,0:T(8,128)}) custom-call(s32[2]{0:T(128)S(1)} %get-tuple-element.60.place_ref, f32[2048,1024]{1,0:T(8,128)} %get-tuple-element.63.refs_0_.refs_1_, bf16[1280,1024]{1,0:T(8,128)(2,1)} %collective-permute-done.5.refs_1_, ...), custom_call_target="tpu_custom_call", output_to_operand_aliasing={{0}: (3, {})} | custom-call | tf_op jit(solution)/shard_map/cond/branch_0_fun/half_rows/pallas_call | solution.py:72
  107.1 7.1 %input_columns.6 = (bf16[512,1024]{1,0:T(8,128)(2,1)}, f32[8,128]{1,0:T(8,128)}) custom-call(s32[2]{0:T(128)S(1)} %get-tuple-element.60.place_ref, bf16[512,1024]{1,0:T(8,128)(2,1)} %collective-permute-done.3.refs_3_.refs_0_, f32[2048,1024]{1,0:T(8,128)} %get-tuple-element.63.refs_0_.refs_1_, bf16[512,1024]{1,0:T(8,128)(2,1)} %collective-permute-done.4.refs_2_, ...), custom_call_target="tpu_custom_call" | custom-call | tf_op jit(solution)/shard_map/cond/branch_0_fun/input_columns/pallas_call | solution.py:72
  114.3 2.1 %collective-permute-start.9 = (bf16[512,1024]{1,0:T(8,128)(2,1)}, bf16[512,1024]{1,0:T(8,128)(2,1)}, u32[]{:S(2)}, u32[]{:S(2)}) collective-permute-start(bf16[512,1024]{1,0:T(8,128)(2,1)} %get-tuple-element.86), channel_id=1, source_target_pairs={{0,2},{2,0},{1,3},{3,1},{4,6},{6,4},{5,7},{7,5},{8,10},{10,8},{9,1... | collective-permute-start | bytes 3145736 | tf_op jit(solution)/shard_map/cond/branch_0_fun/ppermute | solution.py:23
  116.4 1.5 collective-permute-start.13
  117.8 7.2 %input_columns.7 = (bf16[512,1024]{1,0:T(8,128)(2,1)}, f32[8,128]{1,0:T(8,128)}) custom-call(s32[2]{0:T(128)S(1)} %get-tuple-element.60.place_ref, bf16[512,1024]{1,0:T(8,128)(2,1)} %get-tuple-element.66.refs_2_.refs_0_, f32[2048,1024]{1,0:T(8,128)} %get-tuple-element.63.refs_0_.refs_1_, bf16[512,1024]{1,0:T(8,128)(2,1)} %collective-permute-done.refs_2_, ...), custom_call_target="tpu_custom_call" | custom-call | tf_op jit(solution)/shard_map/cond/branch_0_fun/input_columns/pallas_call | solution.py:72
  125.0 14.0 %collective-permute-done.9.refs_2_ = bf16[512,1024]{1,0:T(8,128)(2,1)} collective-permute-done((bf16[512,1024]{1,0:T(8,128)(2,1)}, bf16[512,1024]{1,0:T(8,128)(2,1)}, u32[]{:S(2)}, u32[]{:S(2)}) %collective-permute-start.9) | collective-permute-done | bytes 1048608 | tf_op jit(solution)/shard_map/cond/branch_0_fun/ppermute | solution.py:23
  139.0 1.7 collective-permute-start.12
  141.1 1.0 collective-permute-done.10.refs_3_
  142.0 5.2 %join_columns.3 = (bf16[512,4096]{1,0:T(8,128)(2,1)}, f32[8,128]{1,0:T(8,128)}) custom-call(s32[2]{0:T(128)S(1)} %get-tuple-element.60.place_ref, bf16[512,1024]{1,0:T(8,128)(2,1)} %get-tuple-element.85.refs_0_, bf16[512,1024]{1,0:T(8,128)(2,1)} %collective-permute-done.8.refs_1_, bf16[512,1024]{1,0:T(8,128)(2,1)} %collective-permute-done.9.refs_2_, ...), custom_call_target="tpu_custom_call" | custom-call | tf_op jit(solution)/shard_map/cond/branch_0_fun/join_columns/pallas_call | solution.py:72
  147.2 2.8 %collective-permute-done.14.refs_1_ = bf16[1152,1024]{1,0:T(8,128)(2,1)} collective-permute-done((bf16[1152,1024]{1,0:T(8,128)(2,1)}, bf16[1152,1024]{1,0:T(8,128)(2,1)}, u32[]{:S(2)}, u32[]{:S(2)}) %collective-permute-start.14) | collective-permute-done | bytes 2359328 | tf_op jit(solution)/shard_map/cond/branch_0_fun/ppermute | solution.py:28
  150.0 11.8 %final_rows.12 = (f32[2048,1024]{1,0:T(8,128)}, f32[2048,1024]{1,0:T(8,128)}, f32[8,128]{1,0:T(8,128)}) custom-call(s32[2]{0:T(128)S(1)} %get-tuple-element.60.place_ref, f32[1152,1024]{1,0:T(8,128)} %get-tuple-element.95.refs_0_, bf16[1152,1024]{1,0:T(8,128)(2,1)} %collective-permute-done.14.refs_1_, ...), custom_call_target="tpu_custom_call", output_to_operand_aliasing={{0}: (3, {})} | custom-call | tf_op jit(solution)/shard_map/cond/branch_0_fun/final_rows/pallas_call | solution.py:72
  161.8 16.3 %collective-permute-done.13.refs_1_ = bf16[640,1024]{1,0:T(8,128)(2,1)} collective-permute-done((bf16[640,1024]{1,0:T(8,128)(2,1)}, bf16[640,1024]{1,0:T(8,128)(2,1)}, u32[]{:S(2)}, u32[]{:S(2)}) %collective-permute-start.13) | collective-permute-done | bytes 1310752 | tf_op jit(solution)/shard_map/cond/branch_0_fun/ppermute | solution.py:28
  178.1 7.4 %final_rows.13 = (f32[2048,1024]{1,0:T(8,128)}, f32[2048,1024]{1,0:T(8,128)}, f32[8,128]{1,0:T(8,128)}) custom-call(s32[2]{0:T(128)S(1)} %get-tuple-element.60.place_ref, f32[640,1024]{1,0:T(8,128)} %get-tuple-element.93.refs_0_, bf16[640,1024]{1,0:T(8,128)(2,1)} %collective-permute-done.13.refs_1_, ...), custom_call_target="tpu_custom_call", output_to_operand_aliasing={{0}: (3, {}), {1}: (5, {})} | custom-call | tf_op jit(solution)/shard_map/cond/branch_0_fun/final_rows/pallas_call | solution.py:72
  185.5 2.9 %final_rows.14 = (f32[2048,1024]{1,0:T(8,128)}, f32[2048,1024]{1,0:T(8,128)}, f32[8,128]{1,0:T(8,128)}) custom-call(s32[2]{0:T(128)S(1)} %get-tuple-element.60.place_ref, f32[128,1024]{1,0:T(8,128)} %get-tuple-element.91.refs_0_, bf16[128,1024]{1,0:T(8,128)(2,1)} %collective-permute-done.12.refs_1_, ...), custom_call_target="tpu_custom_call", output_to_operand_aliasing={{0}: (3, {}), {1}: (5, {})} | custom-call | tf_op jit(solution)/shard_map/cond/branch_0_fun/final_rows/pallas_call | solution.py:72
  188.5 2.9 %final_rows.15 = (f32[2048,1024]{1,0:T(8,128)}, f32[2048,1024]{1,0:T(8,128)}, f32[8,128]{1,0:T(8,128)}) custom-call(s32[2]{0:T(128)S(1)} %get-tuple-element.60.place_ref, f32[128,1024]{1,0:T(8,128)} %get-tuple-element.89.refs_0_, bf16[128,1024]{1,0:T(8,128)(2,1)} %collective-permute-done.11.refs_1_, ...), custom_call_target="tpu_custom_call", output_to_operand_aliasing={{0}: (3, {}), {1}: (5, {})} | custom-call | tf_op jit(solution)/shard_map/cond/branch_0_fun/final_rows/pallas_call | solution.py:72
  (21 shorter events, 2.2 us)
Async XLA Ops:
  1.4 3.4 %copy-start = (s32[1,512]{1,0:T(1,128)S(1)}, s32[1,512]{1,0:T(1,128)}, u32[]{:S(2)}) copy-start(s32[1,512]{1,0:T(1,128)} %param.10) | copy-start | bytes 6148
  4.8 38.5 %collective-permute-start.1 = (bf16[768,1024]{1,0:T(8,128)(2,1)}, bf16[768,1024]{1,0:T(8,128)(2,1)}, u32[]{:S(2)}, u32[]{:S(2)}) collective-permute-start(bf16[768,1024]{1,0:T(8,128)(2,1)} %get-tuple-element.67), channel_id=1, source_target_pairs={{0,4},{4,0},{8,12},{12,8},{16,20},{20,16},{24,28},{28,24},{1,5},{5... | collective-permute-start | bytes 4718600 | tf_op jit(solution)/shard_map/cond/branch_0_fun/ppermute | solution.py:28
  19.2 33.3 %collective-permute-start.6 = (bf16[512,1024]{1,0:T(8,128)(2,1)}, bf16[512,1024]{1,0:T(8,128)(2,1)}, u32[]{:S(2)}, u32[]{:S(2)}) collective-permute-start(bf16[512,1024]{1,0:T(8,128)(2,1)} %get-tuple-element.76), channel_id=1, source_target_pairs={{0,2},{2,0},{1,3},{3,1},{4,6},{6,4},{5,7},{7,5},{8,10},{10,8},{9,1... | collective-permute-start | bytes 3145736 | tf_op jit(solution)/shard_map/cond/branch_0_fun/ppermute | solution.py:23
  20.8 78.7 %collective-permute-start.5 = (bf16[1280,1024]{1,0:T(8,128)(2,1)}, bf16[1280,1024]{1,0:T(8,128)(2,1)}, u32[]{:S(2)}, u32[]{:S(2)}) collective-permute-start(bf16[1280,1024]{1,0:T(8,128)(2,1)} %get-tuple-element.73), channel_id=1, source_target_pairs={{0,4},{4,0},{8,12},{12,8},{16,20},{20,16},{24,28},{28,24},{1,5},{5... | collective-permute-start | bytes 7864328 | tf_op jit(solution)/shard_map/cond/branch_0_fun/ppermute | solution.py:28
  21.3 45.4 %collective-permute-start.3 = (bf16[512,1024]{1,0:T(8,128)(2,1)}, bf16[512,1024]{1,0:T(8,128)(2,1)}, u32[]{:S(2)}, u32[]{:S(2)}) collective-permute-start(bf16[512,1024]{1,0:T(8,128)(2,1)} %get-tuple-element.66.refs_2_.refs_0_), channel_id=1, source_target_pairs={{0,2},{2,0},{1,3},{3,1},{4,6},{6,4},{5,7},{7,5},{8,10},{10,8},{9,1... | collective-permute-start | bytes 3145736 | tf_op jit(solution)/shard_map/cond/branch_0_fun/ppermute | solution.py:23
  52.5 54.6 %collective-permute-start.2 = (bf16[1024,1024]{1,0:T(8,128)(2,1)}, bf16[1024,1024]{1,0:T(8,128)(2,1)}, u32[]{:S(2)}, u32[]{:S(2)}) collective-permute-start(bf16[1024,1024]{1,0:T(8,128)(2,1)} %get-tuple-element.72), channel_id=1, source_target_pairs={{0,1},{1,0},{2,3},{3,2},{4,5},{5,4},{6,7},{7,6},{8,9},{9,8},{10,11... | collective-permute-start | bytes 6291464 | tf_op jit(solution)/shard_map/cond/branch_0_fun/ppermute | solution.py:23
  52.5 14.1 %collective-permute-start.7 = (bf16[512,1024]{1,0:T(8,128)(2,1)}, bf16[512,1024]{1,0:T(8,128)(2,1)S(1)}, u32[]{:S(2)}, u32[]{:S(2)}) collective-permute-start(bf16[512,1024]{1,0:T(8,128)(2,1)} %collective-permute-done.6), channel_id=1, source_target_pairs={{0,1},{1,0},{2,3},{3,2},{4,5},{5,4},{6,7},{7,6},{8,9},{9,8},{10,11... | collective-permute-start | bytes 3145736 | tf_op jit(solution)/shard_map/cond/branch_0_fun/ppermute | solution.py:23
  66.6 40.5 %collective-permute-start.4 = (bf16[512,1024]{1,0:T(8,128)(2,1)}, bf16[512,1024]{1,0:T(8,128)(2,1)}, u32[]{:S(2)}, u32[]{:S(2)}) collective-permute-start(bf16[512,1024]{1,0:T(8,128)(2,1)} %collective-permute-done.3.refs_3_.refs_0_), channel_id=1, source_target_pairs={{0,1},{1,0},{2,3},{3,2},{4,5},{5,4},{6,7},{7,6},{8,9},{9,8},{10,11... | collective-permute-start | bytes 3145736 | tf_op jit(solution)/shard_map/cond/branch_0_fun/ppermute | solution.py:23
  82.5 67.5 %collective-permute-start.14 = (bf16[1152,1024]{1,0:T(8,128)(2,1)}, bf16[1152,1024]{1,0:T(8,128)(2,1)}, u32[]{:S(2)}, u32[]{:S(2)}) collective-permute-start(bf16[1152,1024]{1,0:T(8,128)(2,1)} %get-tuple-element.96), channel_id=1, source_target_pairs={{0,4},{4,0},{8,12},{12,8},{16,20},{20,16},{24,28},{28,24},{1,5},{5... | collective-permute-start | bytes 7077896 | tf_op jit(solution)/shard_map/cond/branch_0_fun/ppermute | solution.py:28
  82.8 35.0 %collective-permute-start = (bf16[512,1024]{1,0:T(8,128)(2,1)}, bf16[512,1024]{1,0:T(8,128)(2,1)}, u32[]{:S(2)}, u32[]{:S(2)}) collective-permute-start(bf16[512,1024]{1,0:T(8,128)(2,1)} %get-tuple-element.66.refs_2_.refs_0_), channel_id=1, source_target_pairs={{0,1},{1,0},{2,3},{3,2},{4,5},{5,4},{6,7},{7,6},{8,9},{9,8},{10,11... | collective-permute-start | bytes 3145736 | tf_op jit(solution)/shard_map/cond/branch_0_fun/ppermute | solution.py:23
  114.3 24.8 %collective-permute-start.9 = (bf16[512,1024]{1,0:T(8,128)(2,1)}, bf16[512,1024]{1,0:T(8,128)(2,1)}, u32[]{:S(2)}, u32[]{:S(2)}) collective-permute-start(bf16[512,1024]{1,0:T(8,128)(2,1)} %get-tuple-element.86), channel_id=1, source_target_pairs={{0,2},{2,0},{1,3},{3,1},{4,6},{6,4},{5,7},{7,5},{8,10},{10,8},{9,1... | collective-permute-start | bytes 3145736 | tf_op jit(solution)/shard_map/cond/branch_0_fun/ppermute | solution.py:23
  116.4 61.7 %collective-permute-start.13 = (bf16[640,1024]{1,0:T(8,128)(2,1)}, bf16[640,1024]{1,0:T(8,128)(2,1)}, u32[]{:S(2)}, u32[]{:S(2)}) collective-permute-start(bf16[640,1024]{1,0:T(8,128)(2,1)} %get-tuple-element.94), channel_id=1, source_target_pairs={{0,4},{4,0},{8,12},{12,8},{16,20},{20,16},{24,28},{28,24},{1,5},{5... | collective-permute-start | bytes 3932168 | tf_op jit(solution)/shard_map/cond/branch_0_fun/ppermute | solution.py:28
  125.0 15.7 %collective-permute-start.8 = (bf16[512,1024]{1,0:T(8,128)(2,1)}, bf16[512,1024]{1,0:T(8,128)(2,1)}, u32[]{:S(2)}, u32[]{:S(2)}) collective-permute-start(bf16[512,1024]{1,0:T(8,128)(2,1)} %get-tuple-element.85.refs_0_), channel_id=1, source_target_pairs={{0,1},{1,0},{2,3},{3,2},{4,5},{5,4},{6,7},{7,6},{8,9},{9,8},{10,11... | collective-permute-start | bytes 3145736 | tf_op jit(solution)/shard_map/cond/branch_0_fun/ppermute | solution.py:23
  139.0 3.0 %collective-permute-start.10 = (bf16[512,1024]{1,0:T(8,128)(2,1)}, bf16[512,1024]{1,0:T(8,128)(2,1)}, u32[]{:S(2)}, u32[]{:S(2)}) collective-permute-start(bf16[512,1024]{1,0:T(8,128)(2,1)} %collective-permute-done.9.refs_2_), channel_id=1, source_target_pairs={{0,1},{1,0},{2,3},{3,2},{4,5},{5,4},{6,7},{7,6},{8,9},{9,8},{10,11... | collective-permute-start | bytes 3145736 | tf_op jit(solution)/shard_map/cond/branch_0_fun/ppermute | solution.py:23
  139.0 46.4 %collective-permute-start.12 = (bf16[128,1024]{1,0:T(8,128)(2,1)}, bf16[128,1024]{1,0:T(8,128)(2,1)}, u32[]{:S(2)}, u32[]{:S(2)}) collective-permute-start(bf16[128,1024]{1,0:T(8,128)(2,1)} %get-tuple-element.92), channel_id=1, source_target_pairs={{0,4},{4,0},{8,12},{12,8},{16,20},{20,16},{24,28},{28,24},{1,5},{5... | collective-permute-start | bytes 786440 | tf_op jit(solution)/shard_map/cond/branch_0_fun/ppermute | solution.py:28
  140.7 47.8 %collective-permute-start.11 = (bf16[128,1024]{1,0:T(8,128)(2,1)}, bf16[128,1024]{1,0:T(8,128)(2,1)}, u32[]{:S(2)}, u32[]{:S(2)}) collective-permute-start(bf16[128,1024]{1,0:T(8,128)(2,1)} %get-tuple-element.90), channel_id=1, source_target_pairs={{0,4},{4,0},{8,12},{12,8},{16,20},{20,16},{24,28},{28,24},{1,5},{5... | collective-permute-start | bytes 786440 | tf_op jit(solution)/shard_map/cond/branch_0_fun/ppermute | solution.py:28
